TPU v7x, 128 devices: a whole 4x4x4 slice. The times are simulated.
128 devices in a mesh: expert: 32 (over y_hi, z, x), width: 4 (over y_lo, core).
Axes of the slice: x: 4, y: 4 (y_hi: 2, y_lo: 2; y = y_hi * 2 + y_lo), z: 4, core: 2. Of those that a mesh axis runs over, the one named last changes fastest.
Arguments:
- tokens: bfloat16 [4096, 2880], P('expert', 'width'), may hold values from -6 to 6
- grad_out: bfloat16 [4096, 2880], P('expert', 'width'), may hold values from -6 to 6
- routes: int32 [4096, 4], P('expert'), may hold values from 0 to 127, all different within a row; in each aligned block of 128 rows (0 to 127, 128 to 255, ...) at most 5 rows name the same one
- gates: float32 [4096, 4], P('expert'), may hold values from 0.05 to 1
- ranks: int32 [128], P('expert'), may hold values from 64 to 512
- w_gate: bfloat16 [2880, 2880], P('expert', 'width'), may hold values from -0.109375 to 0.109375
- w_up: bfloat16 [2880, 2880], P('expert', 'width'), may hold values from -0.109375 to 0.109375
- w_down: bfloat16 [2880, 2880], P('width', 'expert'), may hold values from -0.109375 to 0.109375
- delta_in: bfloat16 [128, 2880, 512], P('expert', 'width'), may hold values from -0.109375 to 0.109375
- delta_out: bfloat16 [128, 512, 2, 2880], P('expert', None, None, 'width'), may hold values from -0.25 to 0.25
Outputs:
- grad_tokens: bfloat16 [4096, 2880], P('expert', 'width')
- grad_gate: bfloat16 [2880, 2880], P('expert', 'width')
- grad_up: bfloat16 [2880, 2880], P('expert', 'width')
- grad_down: bfloat16 [2880, 2880], P('width', 'expert')
- grad_delta_in: bfloat16 [128, 2880, 512], P('expert', 'width')
- grad_delta_out: bfloat16 [128, 512, 2, 2880], P('expert', None, None, 'width')
Inputs may be any that keep to these rules, and one draw needn't show every extreme that they name: `routes`: each row names 4 different experts; among the 128 rows of one index of the expert axis (aligned blocks) no expert is named by more than 5 rows, a bound that some block reaches in every draw.
All inputs are finite; a program needn't handle non-finite values.
Results may differ from a plain program's by a relative error of at most 0.03.
Values may be sent and summed in bfloat16 or wider, within the bound.
No kernel may reach another device: no remote copies, remote signals or barrier semaphores. Data moves between devices by JAX's collectives and lax.ppermute only.
A program may use at most 128 MiB of HBM per device.

v0:
```python
import jax
import jax.numpy as jnp
from jax import lax
from jax.experimental import pallas as pl
from jax.experimental.pallas import tpu as pltpu
from jax.sharding import Mesh, PartitionSpec as P

BF = jnp.bfloat16
F32 = jnp.float32
EXPERT = ("yh", "z", "x")
PLANE = ("z", "x")
WIDTH = ("yl", "c")
CAP = 5
HALF = 384
PADDED = 96
WPART = 768
XROWS = 24


def dot(a, b, dims):
    return lax.dot_general(a, b, (dims, ((), ())), preferred_element_type=F32)


def bdot(a, b, dims):
    return lax.dot_general(a, b, (dims, ((0,), (0,))), preferred_element_type=F32)


def targets_of(routes_t, experts):
    flat = routes_t.reshape(1, -1)
    pairs = flat.shape[1]
    onehot = (flat == lax.broadcasted_iota(jnp.int32, (experts, pairs), 0)).astype(BF)
    earlier = lax.broadcasted_iota(jnp.int32, (pairs, pairs), 0) < lax.broadcasted_iota(
        jnp.int32, (pairs, pairs), 1
    )
    before = dot(onehot, earlier.astype(BF), ((1,), (0,)))
    place = jnp.sum(before * onehot.astype(F32), axis=0).astype(jnp.int32)
    return place.reshape(routes_t.shape)


def width_sum(partial, mask, first=None):
    parts = lax.all_to_all(partial.astype(BF), WIDTH, 0, 0)
    total = jnp.sum(parts.astype(F32), axis=0)
    mine = (total * mask).astype(BF)
    if first is not None:
        mine = after(mine, first)
    return lax.all_gather(mine, WIDTH)


def pad_cols(a):
    return jnp.pad(a, ((0, 0),) * (a.ndim - 1) + ((0, 2 * HALF - a.shape[-1]),))


def swap_y(a):
    return lax.ppermute(a, "yh", [(0, 1), (1, 0)])


def pair_kernel(target, gates, base, down, back, pg_out, mixed_out, summed_out, mixed_acc, summed_acc):
    step = pl.program_id(0)
    tile, tokens = back.shape[0], base.shape[0]
    ids = lax.broadcasted_iota(jnp.int32, (tile, tokens), 0) + step * tile
    pick = jnp.zeros((tile, tokens), F32)
    gate = jnp.zeros((tile, tokens), F32)
    for k in range(4):
        hit = target[k : k + 1, :] == ids
        pick = jnp.where(hit, 1.0, pick)
        gate = jnp.where(hit, gates[k : k + 1, :], gate)
    gate = jnp.sum(gate, axis=1, keepdims=True)
    pick = pick.astype(BF)
    pre = dot(pick, base[...], ((1,), (0,))) + back[...].astype(F32)
    pair_down = (gate * dot(pick, down[...], ((1,), (0,)))).astype(BF).astype(F32)
    act, up = pre[:, :HALF], pre[:, HALF:]
    sig = jax.nn.sigmoid(act)
    swish = act * sig
    weighted = (gate * (swish * up)).astype(BF)
    grad_act = (pair_down * up * sig * (1.0 + act * (1.0 - sig))).astype(BF)
    grad_up = (pair_down * swish).astype(BF)
    pg_out[:, :HALF] = grad_act
    pg_out[:, HALF:] = grad_up

    @pl.when(step == 0)
    def _():
        mixed_acc[...] = jnp.zeros_like(mixed_acc)
        summed_acc[...] = jnp.zeros_like(summed_acc)

    mixed_acc[...] += dot(pick, weighted, ((0,), (0,)))
    summed_acc[:, :HALF] += dot(pick, grad_act, ((0,), (0,)))
    summed_acc[:, HALF:] += dot(pick, grad_up, ((0,), (0,)))

    @pl.when(step == pl.num_programs(0) - 1)
    def _():
        mixed_out[...] = mixed_acc[...].astype(BF)
        summed_out[...] = summed_acc[...].astype(BF)


def pair_step(target, gates, base, down, back):
    slots, tokens, tile = back.shape[0], base.shape[0], 320

    def whole(a):
        return pl.BlockSpec(a.shape, lambda i: (0, 0))

    tiled = pl.BlockSpec((tile, 2 * HALF), lambda i: (i, 0))
    sums = [pl.BlockSpec((tokens, n * HALF), lambda i: (0, 0)) for n in (1, 2)]
    return pl.pallas_call(
        pair_kernel,
        grid=(slots // tile,),
        in_specs=[whole(target), whole(gates), whole(base), whole(down), tiled],
        out_specs=[tiled] + sums,
        out_shape=[
            jax.ShapeDtypeStruct((slots, 2 * HALF), BF),
            jax.ShapeDtypeStruct((tokens, HALF), BF),
            jax.ShapeDtypeStruct((tokens, 2 * HALF), BF),
        ],
        scratch_shapes=[pltpu.VMEM((tokens, HALF), F32), pltpu.VMEM((tokens, 2 * HALF), F32)],
        compiler_params=pltpu.CompilerParams(vmem_limit_bytes=40 * 2**20),
        cost_estimate=pl.CostEstimate(
            flops=4 * slots * tokens * 3 * HALF, bytes_accessed=5 * 2**20, transcendentals=slots * HALF
        ),
    )(target, gates, base, down, back)


def one_expert(shape):
    return pl.BlockSpec((1,) + shape[1:], lambda e: (e,) + (0,) * (len(shape) - 1))


def all_of(shape):
    return pl.BlockSpec(shape, lambda e: (0,) * len(shape))


def expert_call(kernel, ins, outs, scratch, flops):
    def spec(shape, split):
        return one_expert(shape) if split else all_of(shape)

    return pl.pallas_call(
        kernel,
        grid=(4,),
        in_specs=[spec(a.shape, split) for a, split in ins],
        out_specs=[spec(shape, split) for shape, split in outs],
        out_shape=[jax.ShapeDtypeStruct(shape, BF) for shape, _ in outs],
        scratch_shapes=scratch,
        compiler_params=pltpu.CompilerParams(vmem_limit_bytes=40 * 2**20),
        cost_estimate=pl.CostEstimate(flops=flops, bytes_accessed=12 * 2**20, transcendentals=0),
    )(*[a for a, _ in ins])


def expert_rows(rows):
    return pl.ds(pl.multiple_of(pl.program_id(0) * rows, 32), rows)


def low_kernel(arrived, perm, factor, rows_out, low_out):
    @pl.when(pl.program_id(0) == 0)
    def _():
        rows_out[...] = dot(perm[...], arrived[...], ((1,), (0,))).astype(BF)

    mine = rows_out[expert_rows(low_out.shape[1]), :]
    low_out[0] = dot(mine, factor[0], ((1,), (0,))).astype(BF)


def pre_kernel(low, factor, perm_t, out, cols):
    step = pl.program_id(0)

    @pl.when(step == 0)
    def _():
        cols[...] = jnp.zeros_like(cols)

    rows = expert_rows(low.shape[1])
    rest = factor.shape[2] - HALF
    for c in range(2):
        pre = dot(low[0], factor[0, c], ((1,), (1,))).astype(BF)
        cols[0, rows, c * HALF : (c + 1) * HALF] = pre[:, :HALF]
        cols[1, rows, c * HALF : c * HALF + rest] = pre[:, HALF:]

    @pl.when(step == pl.num_programs(0) - 1)
    def _():
        for h in range(2):
            out[h] = dot(perm_t[...], cols[h], ((1,), (0,))).astype(BF)


def grad_kernel(arrived, perm, factor, low_out, pg_out):
    @pl.when(pl.program_id(0) == 0)
    def _():
        for h in range(2):
            both = dot(perm[...], arrived[h], ((1,), (0,))).astype(BF)
            for c in range(2):
                pg_out[c, :, h * HALF : (h + 1) * HALF] = both[:, c * HALF : (c + 1) * HALF]

    rows = expert_rows(low_out.shape[1])
    part = factor.shape[2]
    total = dot(pg_out[0, rows, :part], factor[0, 0], ((1,), (0,)))
    total += dot(pg_out[1, rows, :part], factor[0, 1], ((1,), (0,)))
    low_out[0] = total.astype(BF)


def back_kernel(low_grad, factor, perm_t, out, cols):
    step = pl.program_id(0)
    rows = expert_rows(low_grad.shape[1])
    cols[rows, :] = dot(low_grad[0], factor[0], ((1,), (1,))).astype(BF)

    @pl.when(step == pl.num_programs(0) - 1)
    def _():
        out[...] = dot(perm_t[...], cols[...], ((1,), (0,))).astype(BF)


def after(value, first):
    return lax.optimization_barrier((value, first))[0]


def hop(v, axis, k):
    return lax.ppermute(v, axis, [(i, (i + k) % 4) for i in range(4)])


def ring_send(vs, axis, dim):
    at = lax.axis_index(axis)

    def entry(k):
        return jnp.concatenate(
            [lax.dynamic_index_in_dim(v, (at + k) % 4, dim, keepdims=False) for v in vs], axis=-1
        )

    return [entry(0), hop(entry(1), axis, 1), hop(entry(3), axis, 3), entry(2)]


def ring_rest(parts, axis, first=None):
    last = parts[3] if first is None else after(parts[3], first)
    return parts[:3] + [hop(last, axis, 2)]


def ring_total(parts, first):
    parts = after(parts, first)
    return sum((p.astype(F32) for p in parts[1:]), parts[0].astype(F32)).astype(BF)


def local(tokens, grad_out, routes, gates, ranks, w_gate, w_up, w_down, delta_in, delta_out):
    yh = lax.axis_index("yh")
    wi = lax.axis_index("yl") * 2 + lax.axis_index("c")
    rows, part = tokens.shape
    local_e, _, rank_max = delta_in.shape
    n_exp = 32
    experts = n_exp * local_e
    slots = experts * CAP
    er = n_exp * CAP
    wr = w_gate.shape[0]
    rest = part - HALF

    d_id = lax.broadcasted_iota(jnp.int32, (part, WPART), 0)
    j_id = lax.broadcasted_iota(jnp.int32, (part, WPART), 1)
    spread = ((d_id // wr == j_id // PADDED) & (d_id % wr == j_id % PADDED)).astype(BF)

    place = targets_of(routes.T, experts)
    routes_t, gates_t = routes.T, gates.T
    info = jnp.concatenate([(routes_t * 8 + place).astype(F32), gates_t], axis=0)
    target = (routes_t // local_e) * XROWS + (routes_t % local_e) * CAP + place
    slot_ids = lax.broadcasted_iota(jnp.int32, (n_exp * XROWS, rows), 0)
    picker = sum((target[k : k + 1] == slot_ids).astype(F32) for k in range(4)).astype(BF)

    out_x = dot(picker, tokens, ((1,), (0,))).astype(BF).reshape(n_exp, XROWS, part)
    in_x = lax.all_to_all(out_x, EXPERT, 0, 0).reshape(n_exp * XROWS, part)

    xy = jnp.stack([dot(tokens, spread, ((1,), (0,))), dot(grad_out, spread, ((1,), (0,)))]).astype(BF)
    core, low_y = lax.axis_index("c"), lax.axis_index("yl")
    swap = [(0, 1), (1, 0)]

    def pair_up(at, mine, theirs, axis):
        return jnp.where(
            at == 0, jnp.concatenate([mine, theirs], axis=axis), jnp.concatenate([theirs, mine], axis=axis)
        )

    near = pair_up(yh, xy, swap_y(after(xy, out_x)), 1)
    across = lax.ppermute(near, "yl", swap)
    in_x = after(in_x, near)

    far = swap_y(after(info, out_x))
    w3 = jnp.stack([pad_cols(w_gate), pad_cols(w_up), pad_cols(w_down.T)], axis=1)
    w3 = jnp.pad(w3, ((0, PADDED - wr), (0, 0), (0, 0)))
    keep = lax.dynamic_slice_in_dim(w3, yh * HALF, HALF, 2).reshape(PADDED, 3 * HALF)
    give = lax.dynamic_slice_in_dim(w3, (1 - yh) * HALF, HALF, 2).reshape(PADDED, 3 * HALF)
    both_w = lax.all_gather(after(jnp.stack([keep, swap_y(give)]), out_x), PLANE)
    own_w, far_w = [both_w[:, i].reshape(2 * WPART, 3 * HALF) for i in range(2)]

    def order(width, source):
        r = lax.broadcasted_iota(jnp.int32, (slots, width), 0)
        s_in = lax.broadcasted_iota(jnp.int32, (slots, width), 1)
        return (s_in == source(r // er, (r % er) // (2 * CAP), (r % (2 * CAP)) // CAP, r % CAP)).astype(BF)

    perm_x = order(n_exp * XROWS, lambda e, zx, b, p: (b * 16 + zx) * XROWS + e * CAP + p)
    perm_p = order(slots, lambda e, zx, b, p: (zx * 2 + b) * (local_e * CAP) + e * CAP + p)
    factor_out = delta_out.transpose(0, 2, 3, 1)
    rows_x, low_part = expert_call(
        low_kernel,
        [(in_x, False), (perm_x, False), (delta_in, True)],
        [((slots, part), False), ((local_e, er, rank_max), True)],
        [],
        12 * 10**8,
    )
    rows_x = rows_x.reshape(local_e, er, part)
    rank_ids = lax.broadcasted_iota(jnp.int32, (1, rank_max), 1)
    mask = (rank_ids < ranks[wi]).astype(F32)
    low = width_sum(low_part, mask, across)
    [out_pre] = expert_call(
        pre_kernel,
        [(low, True), (factor_out, True), (perm_p.T, False)],
        [((2, slots, 2 * HALF), False)],
        [pltpu.VMEM((2, slots, 2 * HALF), BF)],
        22 * 10**8,
    )
    far = after(far, (both_w, out_pre))
    info2 = jnp.where(
        yh == 0, jnp.concatenate([info, far], axis=1), jnp.concatenate([far, info], axis=1)
    )
    near, across = after((near, across), (both_w, out_pre))
    at_own = low_y == yh
    parts = jnp.stack([jnp.where(at_own, near, across), jnp.where(at_own, across, near)])
    parts = pair_up(core, parts, lax.ppermute(parts, "c", swap), 3)
    own_x, own_y, far_x, far_y = parts[0, 0], parts[0, 1], parts[1, 0], parts[1, 1]
    back_pre = lax.all_to_all(out_pre.reshape(n_exp, 2 * local_e * CAP, 2 * HALF), EXPERT, 0, 0)
    back_pre = back_pre.reshape(2 * slots, 2 * HALF)

    coded = info2[:4].astype(jnp.int32)
    route2, place2 = coded // 8, coded % 8
    block2 = lax.broadcasted_iota(jnp.int32, (4, 2 * rows), 1) // rows
    target2 = ((route2 // local_e) * 2 + block2) * (local_e * CAP) + (route2 % local_e) * CAP + place2

    own_gu, own_d, far_gu, far_d = own_w[:, : 2 * HALF], own_w[:, 2 * HALF :], far_w[:, : 2 * HALF], far_w[:, 2 * HALF :]
    base = (dot(own_x, own_gu, ((1,), (0,))) + dot(far_x, far_gu, ((1,), (0,)))).astype(BF)
    down = (dot(own_y, own_d, ((1,), (0,))) + dot(far_y, far_d, ((1,), (0,)))).astype(BF)
    pair_grad, mixed, summed = pair_step(target2, info2[4:], base, down, back_pre)
    in_p = lax.all_to_all(pair_grad.reshape(n_exp, 2 * local_e * CAP, 2 * HALF), EXPERT, 0, 0)
    in_p = in_p.reshape(2, slots, 2 * HALF)

    def plane_send(feats, axis):
        dws = [
            dot(f, g, ((0,), (0,))).astype(BF).reshape(4, 4, PADDED, -1) for f, g in zip(feats, (summed, mixed))
        ]
        return ring_send(dws, axis, 1 if axis == "x" else 0)

    low_back, pg = expert_call(
        grad_kernel,
        [(in_p, False), (perm_p, False), (factor_out, True)],
        [((local_e, er, rank_max), True), ((2, slots, 2 * HALF), False)],
        [],
        22 * 10**8,
    )
    far_parts = plane_send((far_x, far_y), "x")
    own_parts = plane_send((own_x, own_y), "z")
    low_back = after(low_back, (far_parts[1], far_parts[2], own_parts[1], own_parts[2]))
    far_parts, own_parts = ring_rest(far_parts, "x", low_back), ring_rest(own_parts, "z", low_back)
    low_grad = width_sum(low_back, mask)
    [back] = expert_call(
        back_kernel,
        [(low_grad, True), (delta_in, True), (perm_x.T, False)],
        [((n_exp * XROWS, part), False)],
        [pltpu.VMEM((slots, part), BF)],
        12 * 10**8,
    )
    def dx_part(w, at):
        w_at = lax.dynamic_slice_in_dim(w, at * WPART, WPART, 0)[:, : 2 * HALF]
        return dot(summed, w_at, ((1,), (1,))).astype(BF)

    dx_core = (
        jnp.stack([dx_part(w, core) for w in (own_w, far_w)]),
        lax.ppermute(after(jnp.stack([dx_part(w, 1 - core) for w in (own_w, far_w)]), low_back), "c", swap),
    )
    dx_core = after(dx_core, low_grad)
    dx_own, dx_far = [(dx_core[0][i].astype(F32) + dx_core[1][i].astype(F32)).astype(BF) for i in range(2)]
    dx_keep, dx_give = jnp.where(at_own, dx_own, dx_far), jnp.where(at_own, dx_far, dx_own)
    dx_got = lax.ppermute(dx_give, "yl", swap)
    far_parts = ring_rest(ring_send([ring_total(far_parts, back)], "z", 0), "z")
    own_parts = ring_rest(ring_send([ring_total(own_parts, back)], "x", 0), "x", dx_got)
    sums_done = (far_parts[0], own_parts[0])
    pg = after(pg, sums_done).reshape(2, local_e, er, 2 * HALF)[..., :part]
    grad_delta_out = lax.dot_general(
        low, pg, (((1,), (2,)), ((0,), (1,))), preferred_element_type=F32
    ).astype(BF)
    grad_delta_in = bdot(after(rows_x, sums_done), low_grad, ((1,), (1,))).astype(BF)
    dx = (dx_keep.astype(F32) + dx_got.astype(F32)).astype(BF)
    dx_keep = lax.dynamic_slice_in_dim(dx, yh * rows, rows, 0)
    dx_give = lax.dynamic_slice_in_dim(dx, (1 - yh) * rows, rows, 0)
    dx = dx_keep.astype(F32) + swap_y(dx_give).astype(F32)
    dx_hi = dx.astype(BF)
    dx_lo = (dx - dx_hi.astype(F32)).astype(BF)
    token_grad = dot(dx_hi, spread, ((1,), (1,))) + dot(dx_lo, spread, ((1,), (1,)))

    other = swap_y(ring_total(far_parts, back))
    mine = ring_total(own_parts, back)
    lo = jnp.where(yh == 0, mine, other)[:wr]
    hi = jnp.where(yh == 0, other, mine)[:wr]
    grads = [
        jnp.concatenate([lo[:, i * HALF : (i + 1) * HALF], hi[:, i * HALF : i * HALF + rest]], axis=1)
        for i in range(3)
    ]
    back = lax.all_to_all(back.reshape(n_exp, XROWS, part), EXPERT, 0, 0).reshape(n_exp * XROWS, part)
    grad_tokens = (token_grad + dot(picker, back, ((0,), (0,)))).astype(BF)
    return (grad_tokens, grads[0], grads[1], grads[2].T, grad_delta_in, grad_delta_out)


def solution(mesh):
    fine = Mesh(mesh.devices.reshape(2, 4, 4, 2, 2), ("yh", "z", "x", "yl", "c"))
    return jax.shard_map(
        local,
        mesh=fine,
        in_specs=(
            P(EXPERT, WIDTH),
            P(EXPERT, WIDTH),
            P(EXPERT, None),
            P(EXPERT, None),
            P(EXPERT),
            P(EXPERT, WIDTH),
            P(EXPERT, WIDTH),
            P(WIDTH, EXPERT),
            P(EXPERT, WIDTH, None),
            P(EXPERT, None, None, WIDTH),
        ),
        out_specs=(
            P(EXPERT, WIDTH),
            P(EXPERT, WIDTH),
            P(EXPERT, WIDTH),
            P(WIDTH, EXPERT),
            P(EXPERT, WIDTH, None),
            P(EXPERT, None, None, WIDTH),
        ),
        check_vma=False,
    )
```

profile of v0, /device:TPU:0, one launch (start us, length us, event | category | flops | bytes accessed | tf_op | source)
XLA Modules:
  0.0 297.3 jit_solution(15578850366276627263)
XLA Ops:
  9.3 3.4 %collective-permute-start.1 = (bf16[96,1152]{1,0:T(8,128)(2,1)S(1)}, bf16[96,1152]{1,0:T(8,128)(2,1)S(1)}, u32[]{:S(2)}, u32[]{:S(2)}) collective-permute-start(bf16[96,1152]{1,0:T(8,128)(2,1)S(1)} %bitcast.207), channel_id=1, source_target_pairs={{0,64},{64,0},{1,65},{65,1},{2,66},{66,2},{3,67},{67,3},{4,68},{68... | collective-permute-start | bytes 663560 | tf_op jit(solution)/shard_map/ppermute | solution.py:54
  15.4 2.7 collective-permute-done.1
  19.0 11.1 %all-to-all-start = ((bf16[32,24,720]{2,1,0:T(8,128)(2,1)}), bf16[32,24,720]{2,1,0:T(8,128)(2,1)}, u32[]{:S(2)}, u32[]{:S(2)}) async-start(bf16[32,24,720]{2,1,0:T(8,128)(2,1)} %bitcast.8), calls=%async_computation | async-start | bytes 2359296 | tf_op jit(solution)/shard_map/all_to_all | solution.py:256
  30.1 3.3 %collective-permute-start = (f32[8,128]{1,0:T(8,128)S(1)}, f32[8,128]{1,0:T(8,128)S(1)}, u32[]{:S(2)}, u32[]{:S(2)}) collective-permute-start(f32[8,128]{1,0:T(8,128)S(1)} %pad_maximum_fusion.15), channel_id=1, source_target_pairs={{0,64},{64,0},{1,65},{65,1},{2,66},{66,2},{3,67},{67,3},{4,68},{68... | collective-permute-start | bytes 12296 | tf_op jit(solution)/shard_map/ppermute | solution.py:54
  37.0 4.3 %fusion.30.perm = bf16[640,768]{1,0:T(8,128)(2,1)} fusion(s32[640]{0:T(1024)S(1)} %get-tuple-element.150, s32[640]{0:T(1024)S(1)} %get-tuple-element.156, s32[640]{0:T(1024)S(1)} %get-tuple-element.151, s32[640]{0:T(1024)S(1)} %get-tuple-element.157, s32[640]{0:T(1024)S(1)} %get-tuple-element.152, s32[640]{0:T(1024)S(1)} %get-tuple-element.155, ...), kind=kLoop, calls=%fused_computation.71 | loop fusion | flops 13762560 | bytes 1006080 | tf_op jit(solution)/shard_map/convert_element_type | solution.py:282
  41.3 13.2 %collective-permute-done.2 = bf16[2,128,768]{2,1,0:T(8,128)(2,1)} collective-permute-done((bf16[2,128,768]{2,1,0:T(8,128)(2,1)}, bf16[2,128,768]{2,1,0:T(8,128)(2,1)}, u32[]{:S(2)}, u32[]{:S(2)}) %collective-permute-start.2) | collective-permute-done | bytes 393248 | tf_op jit(solution)/shard_map/ppermute | solution.py:54
  54.5 2.2 maximum_select_fusion.1
  58.7 3.4 %shard_map.145 = (bf16[640,720]{1,0:T(8,128)(2,1)S(1)}, bf16[4,160,512]{2,1,0:T(8,128)(2,1)S(1)}) custom-call(bf16[768,720]{1,0:T(8,128)(2,1)} %bitcast.15.arrived, bf16[640,768]{1,0:T(8,128)(2,1)S(1)} %copy-done.13, bf16[4,720,512]{2,1,0:T(8,128)(2,1)S(1)} %copy-done.4), custom_call_target="tpu_custom_call" | custom-call | flops 1200000000 | bytes 12582912 | tf_op jit(solution)/shard_map/pallas_call | solution.py:133
  63.9 4.3 %all-to-all-start.1 = ((bf16[4,160,512]{2,1,0:T(8,128)(2,1)}), bf16[4,160,512]{2,1,0:T(8,128)(2,1)}, u32[]{:S(2)}, u32[]{:S(2)}) async-start(bf16[4,160,512]{2,1,0:T(8,128)(2,1)} %copy-done.21), calls=%async_computation.1 | async-start | bytes 1310720 | tf_op jit(solution)/shard_map/all_to_all | solution.py:41
  68.2 3.2 %fusion.53 = (bf16[640,640]{1,0:T(8,128)(2,1)}, bf16[640,640]{1,0:T(8,128)(2,1)}) fusion(s32[640]{0:T(1024)S(1)} %get-tuple-element.150, s32[640]{0:T(1024)S(1)} %get-tuple-element.156, s32[640]{0:T(1024)S(1)} %get-tuple-element.151, s32[640]{0:T(1024)S(1)} %get-tuple-element.157, s32[640]{0:T(1024)S(1)} %get-tuple-element.153, ...), kind=kLoop, calls=%fused_computation.96 | loop fusion | flops 22937600 | bytes 1661440 | tf_op jit(solution)/shard_map/convert_element_type | solution.py:282
  72.7 8.7 %all-to-all-done.1 = bf16[4,160,512]{2,1,0:T(8,128)(2,1)} async-done(((bf16[4,160,512]{2,1,0:T(8,128)(2,1)}), bf16[4,160,512]{2,1,0:T(8,128)(2,1)}, u32[]{:S(2)}, u32[]{:S(2)}) %all-to-all-start.1) | async-done | bytes 655392 | tf_op jit(solution)/shard_map/all_to_all | solution.py:41
  82.7 7.2 %all-gather.1 = bf16[640,512]{1,0:T(8,128)(2,1)S(1)} all-gather(bf16[160,512]{1,0:T(8,128)(2,1)S(1)} %multiply_convert_fusion), channel_id=3, replica_groups=mesh['yh'=2,'z'=4,'x'=4,'yl'=2,'c'=2] {'yl','c'}, dimensions={0}, use_global_device_ids=true | all-gather | bytes 819200 | tf_op jit(solution)/shard_map/all_gather | solution.py:46
  90.0 2.7 copy-done.2
  92.6 4.2 %shard_map.146 = bf16[2,640,768]{2,1,0:T(8,128)(2,1)S(1)} custom-call(bf16[4,160,512]{2,1,0:T(8,128)(2,1)S(1)} %bitcast.186, bf16[4,2,720,512]{3,2,1,0:T(8,128)(2,1)S(1)} %bitcast.184, bf16[640,640]{1,0:T(8,128)(2,1)S(1)} %copy-done.16), custom_call_target="tpu_custom_call" | custom-call | flops 2200000000 | bytes 12582912 | tf_op jit(solution)/shard_map/pallas_call | solution.py:133
  103.0 1.7 fusion.27.perm_t
  104.9 8.6 %all-to-all-start.2 = ((bf16[32,40,768]{2,1,0:T(8,128)(2,1)}), bf16[32,40,768]{2,1,0:T(8,128)(2,1)}, u32[]{:S(2)}, u32[]{:S(2)}) async-start(bf16[32,40,768]{2,1,0:T(8,128)(2,1)} %bitcast.188), calls=%async_computation.2 | async-start | bytes 3932160 | tf_op jit(solution)/shard_map/all_to_all | solution.py:314
  113.5 3.8 %fusion.148 = (bf16[16,1,96,1152]{3,2,1,0:T(8,128)(2,1)S(1)}, bf16[16,1,96,1152]{3,2,1,0:T(8,128)(2,1)S(1)}) fusion(bf16[16,2,96,1152]{3,2,1,0:T(8,128)(2,1)} %bitcast.203), kind=kLoop, calls=%fused_computation.317 | loop fusion | bytes 14155776 | tf_op jit(solution)/shard_map/slice | solution.py:277
  117.4 4.6 %maximum_select_fusion = bf16[2,2,256,1536]{3,2,1,0:T(8,128)(2,1)S(1)} fusion(bf16[2,2,256,768]{3,2,1,0:T(8,128)(2,1)} %collective-permute-done.4, bf16[1,2,256,768]{3,2,1,0:T(8,128)(2,1)S(1)} %copy-done.36, bf16[1,2,256,768]{3,2,1,0:T(8,128)(2,1)S(1)} %copy-done.34, pred[]{:T(512)S(6)} %eq.154), kind=kLoop, calls=%fused_computation.15 | loop fusion | flops 20447232 | bytes 6291457 | tf_op jit(solution)/shard_map/jit(_where)/select_n | solution.py:263
  125.6 16.2 %all-to-all-done.2 = bf16[32,40,768]{2,1,0:T(8,128)(2,1)} async-done(((bf16[32,40,768]{2,1,0:T(8,128)(2,1)}), bf16[32,40,768]{2,1,0:T(8,128)(2,1)}, u32[]{:S(2)}, u32[]{:S(2)}) %all-to-all-start.2) | async-done | bytes 1966112 | tf_op jit(solution)/shard_map/all_to_all | solution.py:314
  142.7 6.4 %shard_map.147 = (bf16[1280,768]{1,0:T(8,128)(2,1)S(1)}, bf16[256,384]{1,0:T(8,128)(2,1)S(1)}, bf16[256,768]{1,0:T(8,128)(2,1)S(1)}) custom-call(s32[4,256]{1,0:T(4,128)S(1)} %fusion.129.target, f32[4,256]{1,0:T(4,128)S(1)} %slice.133.gates, bf16[256,768]{1,0:T(8,128)(2,1)S(1)} %copy-done.22, bf16[256,384]{1,0:T(8,128)(2,1)S(1)} %fusion.76.down, ...), custom_call_target="tpu_custom_call" | custom-call | flops 1509949440 | bytes 5242880 | tf_op jit(solution)/shard_map/pallas_call | solution.py:103
  150.7 1.7 convolution_convert_fusion.3
  152.5 2.2 convolution_convert_fusion.1
  154.7 2.3 convolution_convert_fusion
  157.0 5.0 %all-to-all-start.3 = ((bf16[32,40,768]{2,1,0:T(8,128)(2,1)}), bf16[32,40,768]{2,1,0:T(8,128)(2,1)}, u32[]{:S(2)}, u32[]{:S(2)}) async-start(bf16[32,40,768]{2,1,0:T(8,128)(2,1)} %bitcast.191), calls=%async_computation.3 | async-start | bytes 3932160 | tf_op jit(solution)/shard_map/all_to_all | solution.py:326
  165.2 1.7 collective-permute-start.5
  172.3 1.7 collective-permute-start.7
  184.5 6.8 %all-to-all-done.3 = bf16[32,40,768]{2,1,0:T(8,128)(2,1)} async-done(((bf16[32,40,768]{2,1,0:T(8,128)(2,1)}), bf16[32,40,768]{2,1,0:T(8,128)(2,1)}, u32[]{:S(2)}, u32[]{:S(2)}) %all-to-all-start.3) | async-done | bytes 1966112 | tf_op jit(solution)/shard_map/all_to_all | solution.py:326
  191.3 2.7 copy-done.3
  195.1 5.0 %shard_map.148 = (bf16[4,160,512]{2,1,0:T(8,128)(2,1)S(1)}, bf16[2,640,768]{2,1,0:T(8,128)(2,1)S(1)}) custom-call(bf16[2,640,768]{2,1,0:T(8,128)(2,1)} %bitcast.38.arrived, bf16[640,640]{1,0:T(8,128)(2,1)S(1)} %copy-done.15, bf16[4,2,720,512]{3,2,1,0:T(8,128)(2,1)S(1)} %bitcast.185), custom_call_target="tpu_custom_call" | custom-call | flops 2200000000 | bytes 12582912 | tf_op jit(solution)/shard_map/pallas_call | solution.py:133
  202.2 3.1 %collective-permute-done.5 = bf16[4,96,1152]{2,1,0:T(8,128)(2,1)} collective-permute-done((bf16[4,96,1152]{2,1,0:T(8,128)(2,1)}, bf16[4,96,1152]{2,1,0:T(8,128)(2,1)}, u32[]{:S(2)}, u32[]{:S(2)}) %collective-permute-start.5) | collective-permute-done | bytes 884768 | tf_op jit(solution)/shard_map/ppermute | solution.py:208
  206.6 4.2 %all-to-all-start.4 = ((bf16[4,160,512]{2,1,0:T(8,128)(2,1)}), bf16[4,160,512]{2,1,0:T(8,128)(2,1)}, u32[]{:S(2)}, u32[]{:S(2)}) async-start(bf16[4,160,512]{2,1,0:T(8,128)(2,1)} %copy-done.20), calls=%async_computation.4 | async-start | bytes 1310720 | tf_op jit(solution)/shard_map/all_to_all | solution.py:41
  210.8 2.1 pad_maximum_fusion.10
  213.0 2.0 pad_maximum_fusion.6
  216.3 2.5 collective-permute-start.16
  222.4 7.3 %all_gather.20.low_grad = bf16[4,160,512]{2,1,0:T(8,128)(2,1)S(1)} all-gather(bf16[1,160,512]{2,1,0:T(8,128)(2,1)S(1)} %fusion.90), channel_id=1, replica_groups=mesh['yh'=2,'z'=4,'x'=4,'yl'=2,'c'=2] {'yl','c'}, dimensions={0}, use_global_device_ids=true | all-gather | bytes 819200 | tf_op jit(solution)/shard_map/all_gather | solution.py:46
  229.7 2.7 shard_map.149
  233.5 7.7 %all-to-all-start.5 = ((bf16[32,24,720]{2,1,0:T(8,128)(2,1)}), bf16[32,24,720]{2,1,0:T(8,128)(2,1)}, u32[]{:S(2)}, u32[]{:S(2)}) async-start(bf16[32,24,720]{2,1,0:T(8,128)(2,1)} %bitcast.189), calls=%async_computation.5 | async-start | bytes 2359296 | tf_op jit(solution)/shard_map/all_to_all | solution.py:390
  243.2 2.1 add_convert_fusion
  245.4 1.8 collective-permute-start.17
  248.7 2.0 collective-permute-start.19
  250.7 2.3 add_convert_fusion.1
  254.7 4.3 %convolution_convert_fusion.2 = bf16[4,512,2,720]{1,3,2,0:T(8,128)(2,1)} fusion(bf16[4,160,512,1]{2,1,3,0:T(8,128)(2,1)S(1)} %bitcast.187, bf16[2,4,160,768]{3,2,1,0:T(8,128)(2,1)S(1)} %bitcast.190), kind=kOutput, calls=%fused_computation.14 | convolution fusion | flops 946667520 | bytes 8519680 | tf_op jit(solution)/shard_map/dot_general | solution.py:370
  259.0 2.6 convolution_convert_fusion.5
  263.3 7.4 %collective-permute-start.14 = (bf16[96,1152]{1,0:T(8,128)(2,1)S(1)}, bf16[96,1152]{1,0:T(8,128)(2,1)S(1)}, u32[]{:S(2)}, u32[]{:S(2)}) collective-permute-start(bf16[96,1152]{1,0:T(8,128)(2,1)S(1)} %get-tuple-element.109), channel_id=1, source_target_pairs={{0,12},{4,0},{8,4},{12,8},{1,13},{5,1},{9,5},{13,9},{2,14},{6,2},{... | collective-permute-start | bytes 663560 | tf_op jit(solution)/shard_map/ppermute | solution.py:208
  272.4 3.5 %collective-permute-start.20 = (bf16[96,1152]{1,0:T(8,128)(2,1)S(1)}, bf16[96,1152]{1,0:T(8,128)(2,1)S(1)}, u32[]{:S(2)}, u32[]{:S(2)}) collective-permute-start(bf16[96,1152]{1,0:T(8,128)(2,1)S(1)} %add_convert_fusion.4), channel_id=1, source_target_pairs={{0,64},{64,0},{1,65},{65,1},{2,66},{66,2},{3,67},{67,3},{4,68},{68... | collective-permute-start | bytes 663560 | tf_op jit(solution)/shard_map/ppermute | solution.py:54
  277.0 4.5 %collective-permute-done.11 = bf16[128,768]{1,0:T(8,128)(2,1)S(1)} collective-permute-done((bf16[128,768]{1,0:T(8,128)(2,1)S(1)}, bf16[128,768]{1,0:T(8,128)(2,1)S(1)}, u32[]{:S(2)}, u32[]{:S(2)}) %collective-permute-start.11) | collective-permute-done | bytes 196640 | tf_op jit(solution)/shard_map/ppermute | solution.py:54
  282.0 2.0 collective-permute-done.15
  287.4 1.9 fusion.94
  (221 shorter events, 71.8 us)
Async XLA Ops:
  7.2 5.9 %copy-start = (bf16[128,720]{0,1:T(8,128)(2,1)S(1)}, bf16[128,720]{0,1:T(8,128)(2,1)}, u32[]{:S(2)}) copy-start(bf16[128,720]{0,1:T(8,128)(2,1)} %param.10) | copy-start | bytes 552964
  7.2 5.5 %copy-start.52 = (s32[128,4]{0,1:T(4,128)S(1)}, s32[128,4]{0,1:T(4,128)}, u32[]{:S(2)}) copy-start(s32[128,4]{0,1:T(4,128)} %param.12) | copy-start | bytes 6148
  7.2 91.8 %all-gather.4.cloned.1.call-start = ((), (), s32[]{:S(2)}) async-start(), calls=%async_computation.6 | async-start | bytes 7520256 | tf_op jit(solution)/shard_map/all_gather | solution.py:276
  9.3 8.8 %collective-permute-start.1 = (bf16[96,1152]{1,0:T(8,128)(2,1)S(1)}, bf16[96,1152]{1,0:T(8,128)(2,1)S(1)}, u32[]{:S(2)}, u32[]{:S(2)}) collective-permute-start(bf16[96,1152]{1,0:T(8,128)(2,1)S(1)} %bitcast.207), channel_id=1, source_target_pairs={{0,64},{64,0},{1,65},{65,1},{2,66},{66,2},{3,67},{67,3},{4,68},{68... | collective-permute-start | bytes 663560 | tf_op jit(solution)/shard_map/ppermute | solution.py:54
  15.4 14.7 %copy-start.45 = (f32[128,4]{0,1:T(4,128)S(1)}, f32[128,4]{0,1:T(4,128)}, u32[]{:S(2)}) copy-start(f32[128,4]{0,1:T(4,128)} %param.13) | copy-start | bytes 6148
  18.9 16.4 %copy-start.53 = (bf16[128,720]{0,1:T(8,128)(2,1)S(1)}, bf16[128,720]{0,1:T(8,128)(2,1)}, u32[]{:S(2)}) copy-start(bf16[128,720]{0,1:T(8,128)(2,1)} %param.11) | copy-start | bytes 552964
  19.0 38.5 %all-to-all-start = ((bf16[32,24,720]{2,1,0:T(8,128)(2,1)}), bf16[32,24,720]{2,1,0:T(8,128)(2,1)}, u32[]{:S(2)}, u32[]{:S(2)}) async-start(bf16[32,24,720]{2,1,0:T(8,128)(2,1)} %bitcast.8), calls=%async_computation | async-start | bytes 2359296 | tf_op jit(solution)/shard_map/all_to_all | solution.py:256
  30.1 83.3 %collective-permute-start = (f32[8,128]{1,0:T(8,128)S(1)}, f32[8,128]{1,0:T(8,128)S(1)}, u32[]{:S(2)}, u32[]{:S(2)}) collective-permute-start(f32[8,128]{1,0:T(8,128)S(1)} %pad_maximum_fusion.15), channel_id=1, source_target_pairs={{0,64},{64,0},{1,65},{65,1},{2,66},{66,2},{3,67},{67,3},{4,68},{68... | collective-permute-start | bytes 12296 | tf_op jit(solution)/shard_map/ppermute | solution.py:54
  35.8 21.6 %copy-start.4 = (bf16[4,720,512]{2,1,0:T(8,128)(2,1)S(1)}, bf16[4,720,512]{2,1,0:T(8,128)(2,1)}, u32[]{:S(2)}) copy-start(bf16[4,720,512]{2,1,0:T(8,128)(2,1)} %factor.3) | copy-start | bytes 8847364
  36.6 17.8 %collective-permute-start.2 = (bf16[2,128,768]{2,1,0:T(8,128)(2,1)}, bf16[2,128,768]{2,1,0:T(8,128)(2,1)}, u32[]{:S(2)}, u32[]{:S(2)}) collective-permute-start(bf16[2,128,768]{2,1,0:T(8,128)(2,1)} %pad_maximum_fusion.12), channel_id=1, source_target_pairs={{0,64},{64,0},{1,65},{65,1},{2,66},{66,2},{3,67},{67,3},{4,68},{68... | collective-permute-start | bytes 1179656 | tf_op jit(solution)/shard_map/ppermute | solution.py:54
  56.7 26.0 %collective-permute-start.3 = (bf16[2,256,768]{2,1,0:T(8,128)(2,1)}, bf16[2,256,768]{2,1,0:T(8,128)(2,1)}, u32[]{:S(2)}, u32[]{:S(2)}) collective-permute-start(bf16[2,256,768]{2,1,0:T(8,128)(2,1)} %maximum_select_fusion.1), channel_id=1, source_target_pairs={{0,2},{2,0},{1,3},{3,1},{4,6},{6,4},{5,7},{7,5},{8,10},{10,8},{9,1... | collective-permute-start | bytes 2359304 | tf_op jit(solution)/shard_map/ppermute | solution.py:268
  63.9 7.5 %copy-start.54 = (s32[4]{0:T(128)S(1)}, s32[4]{0:T(128)}, u32[]{:S(2)}) copy-start(s32[4]{0:T(128)} %param.14) | copy-start | bytes 52
  63.9 17.5 %all-to-all-start.1 = ((bf16[4,160,512]{2,1,0:T(8,128)(2,1)}), bf16[4,160,512]{2,1,0:T(8,128)(2,1)}, u32[]{:S(2)}, u32[]{:S(2)}) async-start(bf16[4,160,512]{2,1,0:T(8,128)(2,1)} %copy-done.21), calls=%async_computation.1 | async-start | bytes 1310720 | tf_op jit(solution)/shard_map/all_to_all | solution.py:41
  81.4 8.6 %copy-start.16 = (bf16[640,640]{1,0:T(8,128)(2,1)S(1)}, bf16[640,640]{1,0:T(8,128)(2,1)}, u32[]{:S(2)}) copy-start(bf16[640,640]{1,0:T(8,128)(2,1)} %get-tuple-element.125.perm_t) | copy-start | bytes 2457604
  102.7 14.6 %collective-permute-start.4 = (bf16[2,2,256,768]{3,2,1,0:T(8,128)(2,1)}, bf16[2,2,256,768]{3,2,1,0:T(8,128)(2,1)}, u32[]{:S(2)}, u32[]{:S(2)}) collective-permute-start(bf16[2,2,256,768]{3,2,1,0:T(8,128)(2,1)} %pad_maximum_fusion), channel_id=1, source_target_pairs={{0,1},{1,0},{2,3},{3,2},{4,5},{5,4},{6,7},{7,6},{8,9},{9,8},{10,11... | collective-permute-start | bytes 4718600 | tf_op jit(solution)/shard_map/ppermute | solution.py:312
  104.9 36.9 %all-to-all-start.2 = ((bf16[32,40,768]{2,1,0:T(8,128)(2,1)}), bf16[32,40,768]{2,1,0:T(8,128)(2,1)}, u32[]{:S(2)}, u32[]{:S(2)}) async-start(bf16[32,40,768]{2,1,0:T(8,128)(2,1)} %bitcast.188), calls=%async_computation.2 | async-start | bytes 3932160 | tf_op jit(solution)/shard_map/all_to_all | solution.py:314
  117.3 5.9 %copy-start.25 = (bf16[16,1,96,1152]{3,2,1,0:T(8,128)(2,1)}, bf16[16,1,96,1152]{3,2,1,0:T(8,128)(2,1)S(1)}, u32[]{:S(2)}) copy-start(bf16[16,1,96,1152]{3,2,1,0:T(8,128)(2,1)S(1)} %get-tuple-element.89) | copy-start | bytes 10616836
  117.3 6.7 %copy-start.23 = (bf16[16,1,96,1152]{3,2,1,0:T(8,128)(2,1)}, bf16[16,1,96,1152]{3,2,1,0:T(8,128)(2,1)S(1)}, u32[]{:S(2)}) copy-start(bf16[16,1,96,1152]{3,2,1,0:T(8,128)(2,1)S(1)} %get-tuple-element.88) | copy-start | bytes 10616836
  142.7 6.4 %copy-start.30 = (bf16[2,2,256,1536]{3,2,1,0:T(8,128)(2,1)S(1)}, bf16[2,2,256,1536]{3,2,1,0:T(8,128)(2,1)}, u32[]{:S(2)}) copy-start(bf16[2,2,256,1536]{3,2,1,0:T(8,128)(2,1)} %copy-done.29) | copy-start | bytes 9437188
  157.0 34.3 %all-to-all-start.3 = ((bf16[32,40,768]{2,1,0:T(8,128)(2,1)}), bf16[32,40,768]{2,1,0:T(8,128)(2,1)}, u32[]{:S(2)}, u32[]{:S(2)}) async-start(bf16[32,40,768]{2,1,0:T(8,128)(2,1)} %bitcast.191), calls=%async_computation.3 | async-start | bytes 3932160 | tf_op jit(solution)/shard_map/all_to_all | solution.py:326
  165.2 40.2 %collective-permute-start.5 = (bf16[4,96,1152]{2,1,0:T(8,128)(2,1)}, bf16[4,96,1152]{2,1,0:T(8,128)(2,1)}, u32[]{:S(2)}, u32[]{:S(2)}) collective-permute-start(bf16[4,96,1152]{2,1,0:T(8,128)(2,1)} %pad_maximum_fusion.1), channel_id=1, source_target_pairs={{0,4},{4,8},{8,12},{12,0},{1,5},{5,9},{9,13},{13,1},{2,6},{6,10},{... | collective-permute-start | bytes 2654216 | tf_op jit(solution)/shard_map/ppermute | solution.py:208
  167.9 37.5 %collective-permute-start.6 = (bf16[4,96,1152]{2,1,0:T(8,128)(2,1)}, bf16[4,96,1152]{2,1,0:T(8,128)(2,1)}, u32[]{:S(2)}, u32[]{:S(2)}) collective-permute-start(bf16[4,96,1152]{2,1,0:T(8,128)(2,1)} %pad_maximum_fusion.2), channel_id=1, source_target_pairs={{0,12},{4,0},{8,4},{12,8},{1,13},{5,1},{9,5},{13,9},{2,14},{6,2},{... | collective-permute-start | bytes 2654216 | tf_op jit(solution)/shard_map/ppermute | solution.py:208
  170.3 6.3 %copy-start.26 = (bf16[16,1,96,1152]{3,2,1,0:T(8,128)(2,1)S(1)}, bf16[16,1,96,1152]{3,2,1,0:T(8,128)(2,1)}, u32[]{:S(2)}) copy-start(bf16[16,1,96,1152]{3,2,1,0:T(8,128)(2,1)} %copy-done.25) | copy-start | bytes 10616836
  172.3 5.5 %copy-start.24 = (bf16[16,1,96,1152]{3,2,1,0:T(8,128)(2,1)S(1)}, bf16[16,1,96,1152]{3,2,1,0:T(8,128)(2,1)}, u32[]{:S(2)}) copy-start(bf16[16,1,96,1152]{3,2,1,0:T(8,128)(2,1)} %copy-done.23) | copy-start | bytes 10616836
  172.3 34.3 %collective-permute-start.7 = (bf16[4,96,1152]{2,1,0:T(8,128)(2,1)}, bf16[4,96,1152]{2,1,0:T(8,128)(2,1)}, u32[]{:S(2)}, u32[]{:S(2)}) collective-permute-start(bf16[4,96,1152]{2,1,0:T(8,128)(2,1)} %pad_maximum_fusion.3), channel_id=1, source_target_pairs={{0,16},{16,32},{32,48},{48,0},{1,17},{17,33},{33,49},{49,1},{2,18}... | collective-permute-start | bytes 2654216 | tf_op jit(solution)/shard_map/ppermute | solution.py:208
  175.0 31.6 %collective-permute-start.8 = (bf16[4,96,1152]{2,1,0:T(8,128)(2,1)}, bf16[4,96,1152]{2,1,0:T(8,128)(2,1)}, u32[]{:S(2)}, u32[]{:S(2)}) collective-permute-start(bf16[4,96,1152]{2,1,0:T(8,128)(2,1)} %pad_maximum_fusion.4), channel_id=1, source_target_pairs={{0,48},{16,0},{32,16},{48,32},{1,49},{17,1},{33,17},{49,33},{2,50}... | collective-permute-start | bytes 2654216 | tf_op jit(solution)/shard_map/ppermute | solution.py:208
  202.2 10.7 %copy-start.39 = (bf16[4,96,768]{2,1,0:T(8,128)(2,1)S(1)}, bf16[4,96,768]{2,1,0:T(8,128)(2,1)}, u32[]{:S(2)}) copy-start(bf16[4,96,768]{2,1,0:T(8,128)(2,1)} %get-tuple-element.90) | copy-start | bytes 1769476
  206.6 14.5 %all-to-all-start.4 = ((bf16[4,160,512]{2,1,0:T(8,128)(2,1)}), bf16[4,160,512]{2,1,0:T(8,128)(2,1)}, u32[]{:S(2)}, u32[]{:S(2)}) async-start(bf16[4,160,512]{2,1,0:T(8,128)(2,1)} %copy-done.20), calls=%async_computation.4 | async-start | bytes 1310720 | tf_op jit(solution)/shard_map/all_to_all | solution.py:41
  214.9 26.3 %collective-permute-start.9 = (bf16[2,256,768]{2,1,0:T(8,128)(2,1)}, bf16[2,256,768]{2,1,0:T(8,128)(2,1)}, u32[]{:S(2)}, u32[]{:S(2)}) collective-permute-start(bf16[2,256,768]{2,1,0:T(8,128)(2,1)} %pad_maximum_fusion.10), channel_id=1, source_target_pairs={{0,1},{1,0},{2,3},{3,2},{4,5},{5,4},{6,7},{7,6},{8,9},{9,8},{10,11... | collective-permute-start | bytes 2359304 | tf_op jit(solution)/shard_map/ppermute | solution.py:360
  216.3 26.8 %collective-permute-start.16 = (bf16[4,96,1152]{2,1,0:T(8,128)(2,1)}, bf16[4,96,1152]{2,1,0:T(8,128)(2,1)}, u32[]{:S(2)}, u32[]{:S(2)}) collective-permute-start(bf16[4,96,1152]{2,1,0:T(8,128)(2,1)} %pad_maximum_fusion.8), channel_id=1, source_target_pairs={{0,8},{4,12},{8,0},{12,4},{1,9},{5,13},{9,1},{13,5},{2,10},{6,14},... | collective-permute-start | bytes 2654216 | tf_op jit(solution)/shard_map/ppermute | solution.py:208
  218.8 31.9 %collective-permute-start.12 = (bf16[4,96,1152]{2,1,0:T(8,128)(2,1)}, bf16[4,96,1152]{2,1,0:T(8,128)(2,1)}, u32[]{:S(2)}, u32[]{:S(2)}) collective-permute-start(bf16[4,96,1152]{2,1,0:T(8,128)(2,1)} %pad_maximum_fusion.6), channel_id=1, source_target_pairs={{0,32},{16,48},{32,0},{48,16},{1,33},{17,49},{33,1},{49,17},{2,34}... | collective-permute-start | bytes 2654216 | tf_op jit(solution)/shard_map/ppermute | solution.py:208
  221.1 8.6 %copy-start.14 = (bf16[768,640]{1,0:T(8,128)(2,1)S(1)}, bf16[768,640]{1,0:T(8,128)(2,1)}, u32[]{:S(2)}) copy-start(bf16[768,640]{1,0:T(8,128)(2,1)} %fusion.27.perm_t) | copy-start | bytes 2949124
  233.5 7.8 %copy-start.31 = (bf16[2,256,768]{2,1,0:T(8,128)(2,1)S(1)}, bf16[2,256,768]{2,1,0:T(8,128)(2,1)}, u32[]{:S(2)}) copy-start(bf16[2,256,768]{2,1,0:T(8,128)(2,1)} %pad_maximum_fusion.9) | copy-start | bytes 2359300
  233.5 9.7 %copy-start.38 = (bf16[4,96,1152]{2,1,0:T(8,128)(2,1)S(1)}, bf16[4,96,1152]{2,1,0:T(8,128)(2,1)}, u32[]{:S(2)}) copy-start(bf16[4,96,1152]{2,1,0:T(8,128)(2,1)} %pad_maximum_fusion.7) | copy-start | bytes 2654212
  233.5 53.9 %all-to-all-start.5 = ((bf16[32,24,720]{2,1,0:T(8,128)(2,1)}), bf16[32,24,720]{2,1,0:T(8,128)(2,1)}, u32[]{:S(2)}, u32[]{:S(2)}) async-start(bf16[32,24,720]{2,1,0:T(8,128)(2,1)} %bitcast.189), calls=%async_computation.5 | async-start | bytes 2359296 | tf_op jit(solution)/shard_map/all_to_all | solution.py:390
  242.6 28.1 %collective-permute-start.10 = (bf16[256,768]{1,0:T(8,128)(2,1)S(1)}, bf16[256,768]{1,0:T(8,128)(2,1)S(1)}, u32[]{:S(2)}, u32[]{:S(2)}) collective-permute-start(bf16[256,768]{1,0:T(8,128)(2,1)S(1)} %select_bitcast_fusion.2), channel_id=1, source_target_pairs={{0,2},{2,0},{1,3},{3,1},{4,6},{6,4},{5,7},{7,5},{8,10},{10,8},{9,1... | collective-permute-start | bytes 1179656 | tf_op jit(solution)/shard_map/ppermute | solution.py:365
  245.3 5.4 %copy-start.37 = (bf16[4,96,1152]{2,1,0:T(8,128)(2,1)S(1)}, bf16[4,96,1152]{2,1,0:T(8,128)(2,1)}, u32[]{:S(2)}) copy-start(bf16[4,96,1152]{2,1,0:T(8,128)(2,1)} %pad_maximum_fusion.5) | copy-start | bytes 2654212
  245.4 17.9 %collective-permute-start.17 = (bf16[96,1152]{1,0:T(8,128)(2,1)S(1)}, bf16[96,1152]{1,0:T(8,128)(2,1)S(1)}, u32[]{:S(2)}, u32[]{:S(2)}) collective-permute-start(bf16[96,1152]{1,0:T(8,128)(2,1)S(1)} %get-tuple-element.114), channel_id=1, source_target_pairs={{0,16},{16,32},{32,48},{48,0},{1,17},{17,33},{33,49},{49,1},{2,18}... | collective-permute-start | bytes 663560 | tf_op jit(solution)/shard_map/ppermute | solution.py:208
  247.2 23.5 %collective-permute-start.18 = (bf16[96,1152]{1,0:T(8,128)(2,1)S(1)}, bf16[96,1152]{1,0:T(8,128)(2,1)S(1)}, u32[]{:S(2)}, u32[]{:S(2)}) collective-permute-start(bf16[96,1152]{1,0:T(8,128)(2,1)S(1)} %get-tuple-element.113), channel_id=1, source_target_pairs={{0,48},{16,0},{32,16},{48,32},{1,49},{17,1},{33,17},{49,33},{2,50}... | collective-permute-start | bytes 663560 | tf_op jit(solution)/shard_map/ppermute | solution.py:208
  248.7 22.0 %collective-permute-start.19 = (bf16[96,1152]{1,0:T(8,128)(2,1)S(1)}, bf16[96,1152]{1,0:T(8,128)(2,1)S(1)}, u32[]{:S(2)}, u32[]{:S(2)}) collective-permute-start(bf16[96,1152]{1,0:T(8,128)(2,1)S(1)} %get-tuple-element.112), channel_id=1, source_target_pairs={{0,32},{16,48},{32,0},{48,16},{1,33},{17,49},{33,1},{49,17},{2,34}... | collective-permute-start | bytes 663560 | tf_op jit(solution)/shard_map/ppermute | solution.py:208
  253.1 28.9 %collective-permute-start.13 = (bf16[96,1152]{1,0:T(8,128)(2,1)S(1)}, bf16[96,1152]{1,0:T(8,128)(2,1)S(1)}, u32[]{:S(2)}, u32[]{:S(2)}) collective-permute-start(bf16[96,1152]{1,0:T(8,128)(2,1)S(1)} %get-tuple-element.110), channel_id=1, source_target_pairs={{0,4},{4,8},{8,12},{12,0},{1,5},{5,9},{9,13},{13,1},{2,6},{6,10},{... | collective-permute-start | bytes 663560 | tf_op jit(solution)/shard_map/ppermute | solution.py:208
  259.0 11.7 %copy-start.32 = (bf16[2,256,768]{2,1,0:T(8,128)(2,1)S(1)}, bf16[2,256,768]{2,1,0:T(8,128)(2,1)}, u32[]{:S(2)}) copy-start(bf16[2,256,768]{2,1,0:T(8,128)(2,1)} %pad_maximum_fusion.9) | copy-start | bytes 2359300
  261.6 19.9 %copy-start.44 = (pred[720,768]{1,0:T(8,128)(4,1)S(1)}, pred[720,768]{1,0:T(8,128)(4,1)}, u32[]{:S(2)}) copy-start(pred[720,768]{1,0:T(8,128)(4,1)} %copy-done.43) | copy-start | bytes 1658884
  263.3 18.7 %collective-permute-start.14 = (bf16[96,1152]{1,0:T(8,128)(2,1)S(1)}, bf16[96,1152]{1,0:T(8,128)(2,1)S(1)}, u32[]{:S(2)}, u32[]{:S(2)}) collective-permute-start(bf16[96,1152]{1,0:T(8,128)(2,1)S(1)} %get-tuple-element.109), channel_id=1, source_target_pairs={{0,12},{4,0},{8,4},{12,8},{1,13},{5,1},{9,5},{13,9},{2,14},{6,2},{... | collective-permute-start | bytes 663560 | tf_op jit(solution)/shard_map/ppermute | solution.py:208
  272.1 9.4 %collective-permute-start.11 = (bf16[128,768]{1,0:T(8,128)(2,1)S(1)}, bf16[128,768]{1,0:T(8,128)(2,1)S(1)}, u32[]{:S(2)}, u32[]{:S(2)}) collective-permute-start(bf16[128,768]{1,0:T(8,128)(2,1)S(1)} %constant_dynamic-slice_fusion), channel_id=1, source_target_pairs={{0,64},{64,0},{1,65},{65,1},{2,66},{66,2},{3,67},{67,3},{4,68},{68... | collective-permute-start | bytes 589832 | tf_op jit(solution)/shard_map/ppermute | solution.py:54
  272.4 12.7 %collective-permute-start.20 = (bf16[96,1152]{1,0:T(8,128)(2,1)S(1)}, bf16[96,1152]{1,0:T(8,128)(2,1)S(1)}, u32[]{:S(2)}, u32[]{:S(2)}) collective-permute-start(bf16[96,1152]{1,0:T(8,128)(2,1)S(1)} %add_convert_fusion.4), channel_id=1, source_target_pairs={{0,64},{64,0},{1,65},{65,1},{2,66},{66,2},{3,67},{67,3},{4,68},{68... | collective-permute-start | bytes 663560 | tf_op jit(solution)/shard_map/ppermute | solution.py:54
  275.9 8.1 %collective-permute-start.15 = (bf16[96,1152]{1,0:T(8,128)(2,1)S(1)}, bf16[96,1152]{1,0:T(8,128)(2,1)S(1)}, u32[]{:S(2)}, u32[]{:S(2)}) collective-permute-start(bf16[96,1152]{1,0:T(8,128)(2,1)S(1)} %get-tuple-element.68), channel_id=1, source_target_pairs={{0,8},{4,12},{8,0},{12,4},{1,9},{5,13},{9,1},{13,5},{2,10},{6,14},... | collective-permute-start | bytes 663560 | tf_op jit(solution)/shard_map/ppermute | solution.py:208
  282.0 5.4 %copy-start.47 = (s32[128]{0:T(128)S(1)}, s32[128]{0:T(128)}, u32[]{:S(2)}) copy-start(s32[128]{0:T(128)} %copy-done.46) | copy-start | bytes 1540
  (35 other events, 89.9 us)
Sparse Core Ops, SparseCore 0:
  19.1 73.7 all-gather.3
where the time goes:
time: 299 us; the launch traced here: 297 us
  starting transfers between devices  79.2 us (26%)
  waiting for transfers between devices  62.3 us (21%)
  other arithmetic  46.5 us (16%)
  local copies, waits for them, and re-layouts  29.6 us (10%)
  matrix products  28.5 us (10%)
  Pallas kernels  21.7 us (7%)
  between operations  15 us (5%)
  blocking collectives  14.5 us (5%)
    ppermute x12, starting transfers between devices, hop(): return lax.ppermute(v, axis, [(i, (i + k) % 4) for i in range(4)])  25.5 us
    dot_general x19, matrix products, dot(): return lax.dot_general(a, b, (dims, ((), ())), preferred_element_type=F32)  21.6 us
    ppermute x5, waiting for transfers between devices, swap_y(): return lax.ppermute(a, 'yh', [(0, 1), (1, 0)])  21.5 us
    unnamed x110, local copies, waits for them, and re-layouts  17.7 us
    all_to_all x1, waiting for transfers between devices, local(): lax.all_to_all(out_pre.reshape(n_exp, 2 * local_e * CAP, 2 * HALF), EXPER...  16.2 us
    pallas_call x4, Pallas kernels, expert_call(): pl.pallas_call(kernel, grid=(4,), in_specs=[spec(a.shape, split) for a, s...  15.3 us
    all_gather x2, blocking collectives, width_sum(): return lax.all_gather(mine, WIDTH)  14.5 us
    all_to_all x1, starting transfers between devices, local(): in_x = lax.all_to_all(out_x, EXPERT, 0, 0).reshape(n_exp * XROWS, part)  11.1 us
  transfers between devices with their start and end apart: 28, of which 12 were waited for; matrix products, arithmetic and copies ran while one was open for 25% of the time, Pallas kernels for 5%

commit v1 on v0

--- a/solution.py
+++ b/solution.py
@@ -126,7 +126,7 @@
     return pl.BlockSpec(shape, lambda e: (0,) * len(shape))
 
 
-def expert_call(kernel, ins, outs, scratch, flops):
+def expert_call(kernel, ins, outs, scratch, flops, vmem=40):
     def spec(shape, split):
         return one_expert(shape) if split else all_of(shape)
 
@@ -137,7 +137,7 @@
         out_specs=[spec(shape, split) for shape, split in outs],
         out_shape=[jax.ShapeDtypeStruct(shape, BF) for shape, _ in outs],
         scratch_shapes=scratch,
-        compiler_params=pltpu.CompilerParams(vmem_limit_bytes=40 * 2**20),
+        compiler_params=pltpu.CompilerParams(vmem_limit_bytes=vmem * 2**20),
         cost_estimate=pl.CostEstimate(flops=flops, bytes_accessed=12 * 2**20, transcendentals=0),
     )(*[a for a, _ in ins])
 
@@ -301,6 +301,7 @@
         [((2, slots, 2 * HALF), False)],
         [pltpu.VMEM((2, slots, 2 * HALF), BF)],
         22 * 10**8,
+        56,
     )
     far = after(far, (both_w, out_pre))
     info2 = jnp.where(
@@ -338,6 +339,7 @@
         [((local_e, er, rank_max), True), ((2, slots, 2 * HALF), False)],
         [],
         22 * 10**8,
+        56,
     )
     far_parts = plane_send((far_x, far_y), "x")
     own_parts = plane_send((own_x, own_y), "z")

time: 299 us -> 298 us (level)
  local copies, waits for them, and re-layouts: 29.6 us -> 18.9 us
  Pallas kernels: 21.7 us -> 28.4 us
  waiting for transfers between devices: 62.3 us -> 65.3 us
    unnamed x110 -> x94, local copies, waits for them, and re-layouts: 17.7 us -> 6.91 us
    pallas_call x4, Pallas kernels: 15.3 us -> 22.1 us  [expert_call(): pl.pallas_call(kernel, grid=(4,), in_specs=[spec(a.shape, split) for a, s...]
    ppermute x12, waiting for transfers between devices: 8.06 us -> 11.2 us  [hop(): return lax.ppermute(v, axis, [(i, (i + k) % 4) for i in range(4)])]
  transfers between devices with their start and end apart: 28 -> 28, of which waited for: 12 -> 12; matrix products, arithmetic and copies ran while one was open for 25% -> 25% of each run, Pallas kernels for 5% -> 7%
where the time goes in v1:
time: 298 us; the launch traced here: 297 us
  starting transfers between devices  79.2 us (27%)
  waiting for transfers between devices  65.3 us (22%)
  other arithmetic  46.5 us (16%)
  matrix products  28.5 us (10%)
  Pallas kernels  28.4 us (10%)
  local copies, waits for them, and re-layouts  18.9 us (6%)
  blocking collectives  15 us (5%)
  between operations  14.9 us (5%)
    ppermute x12, starting transfers between devices, hop(): return lax.ppermute(v, axis, [(i, (i + k) % 4) for i in range(4)])  25.5 us
    pallas_call x4, Pallas kernels, expert_call(): pl.pallas_call(kernel, grid=(4,), in_specs=[spec(a.shape, split) for a, s...  22.1 us
    dot_general x19, matrix products, dot(): return lax.dot_general(a, b, (dims, ((), ())), preferred_element_type=F32)  21.6 us
    ppermute x5, waiting for transfers between devices, swap_y(): return lax.ppermute(a, 'yh', [(0, 1), (1, 0)])  21.5 us
    all_to_all x1, waiting for transfers between devices, local(): lax.all_to_all(out_pre.reshape(n_exp, 2 * local_e * CAP, 2 * HALF), EXPER...  16.1 us
    all_gather x2, blocking collectives, width_sum(): return lax.all_gather(mine, WIDTH)  15 us
    ppermute x12, waiting for transfers between devices, hop(): return lax.ppermute(v, axis, [(i, (i + k) % 4) for i in range(4)])  11.2 us
    all_to_all x1, starting transfers between devices, local(): in_x = lax.all_to_all(out_x, EXPERT, 0, 0).reshape(n_exp * XROWS, part)  11.1 us
  transfers between devices with their start and end apart: 28, of which 12 were waited for; matrix products, arithmetic and copies ran while one was open for 25% of the time, Pallas kernels for 7%

profile of v1, /device:TPU:0, one launch (start us, length us, event | category | flops | bytes accessed | tf_op | source)
XLA Modules:
  0.0 296.7 jit_solution(12234475995148476229)
XLA Ops:
  9.3 3.4 %collective-permute-start.1 = (bf16[96,1152]{1,0:T(8,128)(2,1)S(1)}, bf16[96,1152]{1,0:T(8,128)(2,1)S(1)}, u32[]{:S(2)}, u32[]{:S(2)}) collective-permute-start(bf16[96,1152]{1,0:T(8,128)(2,1)S(1)} %bitcast.207), channel_id=1, source_target_pairs={{0,64},{64,0},{1,65},{65,1},{2,66},{66,2},{3,67},{67,3},{4,68},{68... | collective-permute-start | bytes 663560 | tf_op jit(solution)/shard_map/ppermute | solution.py:54
  15.4 2.7 collective-permute-done.1
  19.0 11.1 %all-to-all-start = ((bf16[32,24,720]{2,1,0:T(8,128)(2,1)}), bf16[32,24,720]{2,1,0:T(8,128)(2,1)}, u32[]{:S(2)}, u32[]{:S(2)}) async-start(bf16[32,24,720]{2,1,0:T(8,128)(2,1)} %bitcast.8), calls=%async_computation | async-start | bytes 2359296 | tf_op jit(solution)/shard_map/all_to_all | solution.py:256
  30.1 3.3 %collective-permute-start = (f32[8,128]{1,0:T(8,128)S(1)}, f32[8,128]{1,0:T(8,128)S(1)}, u32[]{:S(2)}, u32[]{:S(2)}) collective-permute-start(f32[8,128]{1,0:T(8,128)S(1)} %pad_maximum_fusion.15), channel_id=1, source_target_pairs={{0,64},{64,0},{1,65},{65,1},{2,66},{66,2},{3,67},{67,3},{4,68},{68... | collective-permute-start | bytes 12296 | tf_op jit(solution)/shard_map/ppermute | solution.py:54
  37.0 4.3 %fusion.30.perm = bf16[640,768]{1,0:T(8,128)(2,1)} fusion(s32[640]{0:T(1024)S(1)} %get-tuple-element.150, s32[640]{0:T(1024)S(1)} %get-tuple-element.156, s32[640]{0:T(1024)S(1)} %get-tuple-element.151, s32[640]{0:T(1024)S(1)} %get-tuple-element.157, s32[640]{0:T(1024)S(1)} %get-tuple-element.152, s32[640]{0:T(1024)S(1)} %get-tuple-element.155, ...), kind=kLoop, calls=%fused_computation.71 | loop fusion | flops 13762560 | bytes 1006080 | tf_op jit(solution)/shard_map/convert_element_type | solution.py:282
  41.3 13.2 %collective-permute-done.2 = bf16[2,128,768]{2,1,0:T(8,128)(2,1)} collective-permute-done((bf16[2,128,768]{2,1,0:T(8,128)(2,1)}, bf16[2,128,768]{2,1,0:T(8,128)(2,1)}, u32[]{:S(2)}, u32[]{:S(2)}) %collective-permute-start.2) | collective-permute-done | bytes 393248 | tf_op jit(solution)/shard_map/ppermute | solution.py:54
  54.5 2.3 maximum_select_fusion.1
  58.7 3.4 %shard_map.145 = (bf16[640,720]{1,0:T(8,128)(2,1)S(1)}, bf16[4,160,512]{2,1,0:T(8,128)(2,1)S(1)}) custom-call(bf16[768,720]{1,0:T(8,128)(2,1)} %bitcast.15.arrived, bf16[640,768]{1,0:T(8,128)(2,1)S(1)} %copy-done.6, bf16[4,720,512]{2,1,0:T(8,128)(2,1)S(1)} %copy-done.2), custom_call_target="tpu_custom_call" | custom-call | flops 1200000000 | bytes 12582912 | tf_op jit(solution)/shard_map/pallas_call | solution.py:133
  63.9 4.3 %all-to-all-start.1 = ((bf16[4,160,512]{2,1,0:T(8,128)(2,1)}), bf16[4,160,512]{2,1,0:T(8,128)(2,1)}, u32[]{:S(2)}, u32[]{:S(2)}) async-start(bf16[4,160,512]{2,1,0:T(8,128)(2,1)} %copy-done.11), calls=%async_computation.1 | async-start | bytes 1310720 | tf_op jit(solution)/shard_map/all_to_all | solution.py:41
  68.2 3.2 %fusion.53 = (bf16[640,640]{1,0:T(8,128)(2,1)}, bf16[640,640]{1,0:T(8,128)(2,1)}) fusion(s32[640]{0:T(1024)S(1)} %get-tuple-element.150, s32[640]{0:T(1024)S(1)} %get-tuple-element.156, s32[640]{0:T(1024)S(1)} %get-tuple-element.151, s32[640]{0:T(1024)S(1)} %get-tuple-element.157, s32[640]{0:T(1024)S(1)} %get-tuple-element.153, ...), kind=kLoop, calls=%fused_computation.96 | loop fusion | flops 22937600 | bytes 1661440 | tf_op jit(solution)/shard_map/convert_element_type | solution.py:282
  72.7 8.7 %all-to-all-done.1 = bf16[4,160,512]{2,1,0:T(8,128)(2,1)} async-done(((bf16[4,160,512]{2,1,0:T(8,128)(2,1)}), bf16[4,160,512]{2,1,0:T(8,128)(2,1)}, u32[]{:S(2)}, u32[]{:S(2)}) %all-to-all-start.1) | async-done | bytes 655392 | tf_op jit(solution)/shard_map/all_to_all | solution.py:41
  82.7 7.7 %all-gather.1 = bf16[640,512]{1,0:T(8,128)(2,1)} all-gather(bf16[160,512]{1,0:T(8,128)(2,1)S(1)} %multiply_convert_fusion), channel_id=3, replica_groups=mesh['yh'=2,'z'=4,'x'=4,'yl'=2,'c'=2] {'yl','c'}, dimensions={0}, use_global_device_ids=true | all-gather | bytes 819200 | tf_op jit(solution)/shard_map/all_gather | solution.py:46
  90.3 8.1 %shard_map.146 = bf16[2,640,768]{2,1,0:T(8,128)(2,1)} custom-call(bf16[4,160,512]{2,1,0:T(8,128)(2,1)} %bitcast.199, bf16[4,2,720,512]{3,2,1,0:T(8,128)(2,1)} %bitcast.187, bf16[640,640]{1,0:T(8,128)(2,1)} %get-tuple-element.125.perm_t), custom_call_target="tpu_custom_call" | custom-call | flops 2200000000 | bytes 12582912 | tf_op jit(solution)/shard_map/pallas_call | solution.py:133
  102.5 1.7 fusion.27.perm_t
  104.3 8.6 %all-to-all-start.2 = ((bf16[32,40,768]{2,1,0:T(8,128)(2,1)}), bf16[32,40,768]{2,1,0:T(8,128)(2,1)}, u32[]{:S(2)}, u32[]{:S(2)}) async-start(bf16[32,40,768]{2,1,0:T(8,128)(2,1)} %bitcast.201), calls=%async_computation.2 | async-start | bytes 3932160 | tf_op jit(solution)/shard_map/all_to_all | solution.py:315
  113.0 3.8 %fusion.148 = (bf16[16,1,96,1152]{3,2,1,0:T(8,128)(2,1)S(1)}, bf16[16,1,96,1152]{3,2,1,0:T(8,128)(2,1)S(1)}) fusion(bf16[16,2,96,1152]{3,2,1,0:T(8,128)(2,1)} %bitcast.202), kind=kLoop, calls=%fused_computation.317 | loop fusion | bytes 14155776 | tf_op jit(solution)/shard_map/slice | solution.py:277
  116.9 4.6 %maximum_select_fusion = bf16[2,2,256,1536]{3,2,1,0:T(8,128)(2,1)S(1)} fusion(bf16[2,2,256,768]{3,2,1,0:T(8,128)(2,1)} %collective-permute-done.4, bf16[1,2,256,768]{3,2,1,0:T(8,128)(2,1)S(1)} %copy-done.27, bf16[1,2,256,768]{3,2,1,0:T(8,128)(2,1)S(1)} %copy-done.25, pred[]{:T(512)S(6)} %eq.154), kind=kLoop, calls=%fused_computation.15 | loop fusion | flops 20447232 | bytes 6291457 | tf_op jit(solution)/shard_map/jit(_where)/select_n | solution.py:263
  125.1 16.1 %all-to-all-done.2 = bf16[32,40,768]{2,1,0:T(8,128)(2,1)} async-done(((bf16[32,40,768]{2,1,0:T(8,128)(2,1)}), bf16[32,40,768]{2,1,0:T(8,128)(2,1)}, u32[]{:S(2)}, u32[]{:S(2)}) %all-to-all-start.2) | async-done | bytes 1966112 | tf_op jit(solution)/shard_map/all_to_all | solution.py:315
  142.2 6.4 %shard_map.147 = (bf16[1280,768]{1,0:T(8,128)(2,1)S(1)}, bf16[256,384]{1,0:T(8,128)(2,1)S(1)}, bf16[256,768]{1,0:T(8,128)(2,1)S(1)}) custom-call(s32[4,256]{1,0:T(4,128)S(1)} %fusion.129.target, f32[4,256]{1,0:T(4,128)S(1)} %slice.133.gates, bf16[256,768]{1,0:T(8,128)(2,1)S(1)} %copy-done.12, bf16[256,384]{1,0:T(8,128)(2,1)S(1)} %fusion.76.down, ...), custom_call_target="tpu_custom_call" | custom-call | flops 1509949440 | bytes 5242880 | tf_op jit(solution)/shard_map/pallas_call | solution.py:103
  148.6 1.6 convolution_convert_fusion.4
  150.2 1.7 convolution_convert_fusion.3
  151.9 2.2 convolution_convert_fusion.1
  154.2 2.3 convolution_convert_fusion
  156.4 5.0 %all-to-all-start.3 = ((bf16[32,40,768]{2,1,0:T(8,128)(2,1)}), bf16[32,40,768]{2,1,0:T(8,128)(2,1)}, u32[]{:S(2)}, u32[]{:S(2)}) async-start(bf16[32,40,768]{2,1,0:T(8,128)(2,1)} %bitcast.185), calls=%async_computation.3 | async-start | bytes 3932160 | tf_op jit(solution)/shard_map/all_to_all | solution.py:327
  164.6 1.7 collective-permute-start.5
  171.7 1.7 collective-permute-start.7
  184.0 6.8 %all-to-all-done.3 = bf16[32,40,768]{2,1,0:T(8,128)(2,1)} async-done(((bf16[32,40,768]{2,1,0:T(8,128)(2,1)}), bf16[32,40,768]{2,1,0:T(8,128)(2,1)}, u32[]{:S(2)}, u32[]{:S(2)}) %all-to-all-start.3) | async-done | bytes 1966112 | tf_op jit(solution)/shard_map/all_to_all | solution.py:327
  190.8 7.8 %shard_map.148 = (bf16[4,160,512]{2,1,0:T(8,128)(2,1)}, bf16[2,640,768]{2,1,0:T(8,128)(2,1)}) custom-call(bf16[2,640,768]{2,1,0:T(8,128)(2,1)} %bitcast.38.arrived, bf16[640,640]{1,0:T(8,128)(2,1)} %get-tuple-element.124.perm, bf16[4,2,720,512]{3,2,1,0:T(8,128)(2,1)} %bitcast.188), custom_call_target="tpu_custom_call" | custom-call | flops 2200000000 | bytes 12582912 | tf_op jit(solution)/shard_map/pallas_call | solution.py:133
  198.6 6.2 %collective-permute-done.5 = bf16[4,96,1152]{2,1,0:T(8,128)(2,1)} collective-permute-done((bf16[4,96,1152]{2,1,0:T(8,128)(2,1)}, bf16[4,96,1152]{2,1,0:T(8,128)(2,1)}, u32[]{:S(2)}, u32[]{:S(2)}) %collective-permute-start.5) | collective-permute-done | bytes 884768 | tf_op jit(solution)/shard_map/ppermute | solution.py:208
  206.0 4.2 %all-to-all-start.4 = ((bf16[4,160,512]{2,1,0:T(8,128)(2,1)}), bf16[4,160,512]{2,1,0:T(8,128)(2,1)}, u32[]{:S(2)}, u32[]{:S(2)}) async-start(bf16[4,160,512]{2,1,0:T(8,128)(2,1)} %get-tuple-element.59), calls=%async_computation.4 | async-start | bytes 1310720 | tf_op jit(solution)/shard_map/all_to_all | solution.py:41
  210.2 2.1 pad_maximum_fusion.10
  212.4 2.0 pad_maximum_fusion.6
  215.8 2.5 collective-permute-start.16
  221.8 7.3 %all_gather.20.low_grad = bf16[4,160,512]{2,1,0:T(8,128)(2,1)S(1)} all-gather(bf16[1,160,512]{2,1,0:T(8,128)(2,1)S(1)} %fusion.90), channel_id=1, replica_groups=mesh['yh'=2,'z'=4,'x'=4,'yl'=2,'c'=2] {'yl','c'}, dimensions={0}, use_global_device_ids=true | all-gather | bytes 819200 | tf_op jit(solution)/shard_map/all_gather | solution.py:46
  229.1 2.7 shard_map.149
  232.9 7.7 %all-to-all-start.5 = ((bf16[32,24,720]{2,1,0:T(8,128)(2,1)}), bf16[32,24,720]{2,1,0:T(8,128)(2,1)}, u32[]{:S(2)}, u32[]{:S(2)}) async-start(bf16[32,24,720]{2,1,0:T(8,128)(2,1)} %bitcast.184), calls=%async_computation.5 | async-start | bytes 2359296 | tf_op jit(solution)/shard_map/all_to_all | solution.py:392
  242.6 2.1 add_convert_fusion
  244.8 1.8 collective-permute-start.17
  248.1 2.0 collective-permute-start.19
  250.1 2.3 add_convert_fusion.1
  254.1 4.3 %convolution_convert_fusion.2 = bf16[4,512,2,720]{1,3,2,0:T(8,128)(2,1)} fusion(bf16[4,160,512,1]{2,1,3,0:T(8,128)(2,1)S(1)} %bitcast.200, bf16[2,4,160,768]{3,2,1,0:T(8,128)(2,1)S(1)} %bitcast.203), kind=kOutput, calls=%fused_computation.14 | convolution fusion | flops 946667520 | bytes 8519680 | tf_op jit(solution)/shard_map/dot_general | solution.py:372
  258.4 2.6 convolution_convert_fusion.5
  261.0 1.7 collective-permute-done.17
  262.7 7.4 %collective-permute-start.14 = (bf16[96,1152]{1,0:T(8,128)(2,1)S(1)}, bf16[96,1152]{1,0:T(8,128)(2,1)S(1)}, u32[]{:S(2)}, u32[]{:S(2)}) collective-permute-start(bf16[96,1152]{1,0:T(8,128)(2,1)S(1)} %get-tuple-element.109), channel_id=1, source_target_pairs={{0,12},{4,0},{8,4},{12,8},{1,13},{5,1},{9,5},{13,9},{2,14},{6,2},{... | collective-permute-start | bytes 663560 | tf_op jit(solution)/shard_map/ppermute | solution.py:208
  271.8 3.5 %collective-permute-start.20 = (bf16[96,1152]{1,0:T(8,128)(2,1)S(1)}, bf16[96,1152]{1,0:T(8,128)(2,1)S(1)}, u32[]{:S(2)}, u32[]{:S(2)}) collective-permute-start(bf16[96,1152]{1,0:T(8,128)(2,1)S(1)} %add_convert_fusion.4), channel_id=1, source_target_pairs={{0,64},{64,0},{1,65},{65,1},{2,66},{66,2},{3,67},{67,3},{4,68},{68... | collective-permute-start | bytes 663560 | tf_op jit(solution)/shard_map/ppermute | solution.py:54
  276.4 4.5 %collective-permute-done.11 = bf16[128,768]{1,0:T(8,128)(2,1)S(1)} collective-permute-done((bf16[128,768]{1,0:T(8,128)(2,1)S(1)}, bf16[128,768]{1,0:T(8,128)(2,1)S(1)}, u32[]{:S(2)}, u32[]{:S(2)}) %collective-permute-start.11) | collective-permute-done | bytes 196640 | tf_op jit(solution)/shard_map/ppermute | solution.py:54
  281.4 2.0 collective-permute-done.15
  286.8 1.9 fusion.94
  (205 shorter events, 63.0 us)
Async XLA Ops:
  7.2 5.9 %copy-start = (bf16[128,720]{0,1:T(8,128)(2,1)S(1)}, bf16[128,720]{0,1:T(8,128)(2,1)}, u32[]{:S(2)}) copy-start(bf16[128,720]{0,1:T(8,128)(2,1)} %param.10) | copy-start | bytes 552964
  7.2 5.5 %copy-start.44 = (s32[128,4]{0,1:T(4,128)S(1)}, s32[128,4]{0,1:T(4,128)}, u32[]{:S(2)}) copy-start(s32[128,4]{0,1:T(4,128)} %param.12) | copy-start | bytes 6148
  7.2 91.3 %all-gather.4.cloned.1.call-start = ((), (), s32[]{:S(2)}) async-start(), calls=%async_computation.6 | async-start | bytes 7520256 | tf_op jit(solution)/shard_map/all_gather | solution.py:276
  9.3 8.8 %collective-permute-start.1 = (bf16[96,1152]{1,0:T(8,128)(2,1)S(1)}, bf16[96,1152]{1,0:T(8,128)(2,1)S(1)}, u32[]{:S(2)}, u32[]{:S(2)}) collective-permute-start(bf16[96,1152]{1,0:T(8,128)(2,1)S(1)} %bitcast.207), channel_id=1, source_target_pairs={{0,64},{64,0},{1,65},{65,1},{2,66},{66,2},{3,67},{67,3},{4,68},{68... | collective-permute-start | bytes 663560 | tf_op jit(solution)/shard_map/ppermute | solution.py:54
  15.4 14.7 %copy-start.37 = (f32[128,4]{0,1:T(4,128)S(1)}, f32[128,4]{0,1:T(4,128)}, u32[]{:S(2)}) copy-start(f32[128,4]{0,1:T(4,128)} %param.13) | copy-start | bytes 6148
  19.0 16.4 %copy-start.45 = (bf16[128,720]{0,1:T(8,128)(2,1)S(1)}, bf16[128,720]{0,1:T(8,128)(2,1)}, u32[]{:S(2)}) copy-start(bf16[128,720]{0,1:T(8,128)(2,1)} %param.11) | copy-start | bytes 552964
  19.0 38.5 %all-to-all-start = ((bf16[32,24,720]{2,1,0:T(8,128)(2,1)}), bf16[32,24,720]{2,1,0:T(8,128)(2,1)}, u32[]{:S(2)}, u32[]{:S(2)}) async-start(bf16[32,24,720]{2,1,0:T(8,128)(2,1)} %bitcast.8), calls=%async_computation | async-start | bytes 2359296 | tf_op jit(solution)/shard_map/all_to_all | solution.py:256
  30.1 82.8 %collective-permute-start = (f32[8,128]{1,0:T(8,128)S(1)}, f32[8,128]{1,0:T(8,128)S(1)}, u32[]{:S(2)}, u32[]{:S(2)}) collective-permute-start(f32[8,128]{1,0:T(8,128)S(1)} %pad_maximum_fusion.15), channel_id=1, source_target_pairs={{0,64},{64,0},{1,65},{65,1},{2,66},{66,2},{3,67},{67,3},{4,68},{68... | collective-permute-start | bytes 12296 | tf_op jit(solution)/shard_map/ppermute | solution.py:54
  35.8 21.7 %copy-start.2 = (bf16[4,720,512]{2,1,0:T(8,128)(2,1)S(1)}, bf16[4,720,512]{2,1,0:T(8,128)(2,1)}, u32[]{:S(2)}) copy-start(bf16[4,720,512]{2,1,0:T(8,128)(2,1)} %factor.3) | copy-start | bytes 8847364
  36.6 17.9 %collective-permute-start.2 = (bf16[2,128,768]{2,1,0:T(8,128)(2,1)}, bf16[2,128,768]{2,1,0:T(8,128)(2,1)}, u32[]{:S(2)}, u32[]{:S(2)}) collective-permute-start(bf16[2,128,768]{2,1,0:T(8,128)(2,1)} %pad_maximum_fusion.12), channel_id=1, source_target_pairs={{0,64},{64,0},{1,65},{65,1},{2,66},{66,2},{3,67},{67,3},{4,68},{68... | collective-permute-start | bytes 1179656 | tf_op jit(solution)/shard_map/ppermute | solution.py:54
  56.7 25.9 %collective-permute-start.3 = (bf16[2,256,768]{2,1,0:T(8,128)(2,1)}, bf16[2,256,768]{2,1,0:T(8,128)(2,1)}, u32[]{:S(2)}, u32[]{:S(2)}) collective-permute-start(bf16[2,256,768]{2,1,0:T(8,128)(2,1)} %maximum_select_fusion.1), channel_id=1, source_target_pairs={{0,2},{2,0},{1,3},{3,1},{4,6},{6,4},{5,7},{7,5},{8,10},{10,8},{9,1... | collective-permute-start | bytes 2359304 | tf_op jit(solution)/shard_map/ppermute | solution.py:268
  63.9 7.5 %copy-start.46 = (s32[4]{0:T(128)S(1)}, s32[4]{0:T(128)}, u32[]{:S(2)}) copy-start(s32[4]{0:T(128)} %param.14) | copy-start | bytes 52
  63.9 17.5 %all-to-all-start.1 = ((bf16[4,160,512]{2,1,0:T(8,128)(2,1)}), bf16[4,160,512]{2,1,0:T(8,128)(2,1)}, u32[]{:S(2)}, u32[]{:S(2)}) async-start(bf16[4,160,512]{2,1,0:T(8,128)(2,1)} %copy-done.11), calls=%async_computation.1 | async-start | bytes 1310720 | tf_op jit(solution)/shard_map/all_to_all | solution.py:41
  102.2 14.7 %collective-permute-start.4 = (bf16[2,2,256,768]{3,2,1,0:T(8,128)(2,1)}, bf16[2,2,256,768]{3,2,1,0:T(8,128)(2,1)}, u32[]{:S(2)}, u32[]{:S(2)}) collective-permute-start(bf16[2,2,256,768]{3,2,1,0:T(8,128)(2,1)} %pad_maximum_fusion), channel_id=1, source_target_pairs={{0,1},{1,0},{2,3},{3,2},{4,5},{5,4},{6,7},{7,6},{8,9},{9,8},{10,11... | collective-permute-start | bytes 4718600 | tf_op jit(solution)/shard_map/ppermute | solution.py:313
  104.3 36.9 %all-to-all-start.2 = ((bf16[32,40,768]{2,1,0:T(8,128)(2,1)}), bf16[32,40,768]{2,1,0:T(8,128)(2,1)}, u32[]{:S(2)}, u32[]{:S(2)}) async-start(bf16[32,40,768]{2,1,0:T(8,128)(2,1)} %bitcast.201), calls=%async_computation.2 | async-start | bytes 3932160 | tf_op jit(solution)/shard_map/all_to_all | solution.py:315
  116.8 5.9 %copy-start.15 = (bf16[16,1,96,1152]{3,2,1,0:T(8,128)(2,1)}, bf16[16,1,96,1152]{3,2,1,0:T(8,128)(2,1)S(1)}, u32[]{:S(2)}) copy-start(bf16[16,1,96,1152]{3,2,1,0:T(8,128)(2,1)S(1)} %get-tuple-element.89) | copy-start | bytes 10616836
  116.8 6.7 %copy-start.13 = (bf16[16,1,96,1152]{3,2,1,0:T(8,128)(2,1)}, bf16[16,1,96,1152]{3,2,1,0:T(8,128)(2,1)S(1)}, u32[]{:S(2)}) copy-start(bf16[16,1,96,1152]{3,2,1,0:T(8,128)(2,1)S(1)} %get-tuple-element.88) | copy-start | bytes 10616836
  142.2 6.4 %copy-start.21 = (bf16[2,2,256,1536]{3,2,1,0:T(8,128)(2,1)S(1)}, bf16[2,2,256,1536]{3,2,1,0:T(8,128)(2,1)}, u32[]{:S(2)}) copy-start(bf16[2,2,256,1536]{3,2,1,0:T(8,128)(2,1)} %copy-done.20) | copy-start | bytes 9437188
  156.4 34.4 %all-to-all-start.3 = ((bf16[32,40,768]{2,1,0:T(8,128)(2,1)}), bf16[32,40,768]{2,1,0:T(8,128)(2,1)}, u32[]{:S(2)}, u32[]{:S(2)}) async-start(bf16[32,40,768]{2,1,0:T(8,128)(2,1)} %bitcast.185), calls=%async_computation.3 | async-start | bytes 3932160 | tf_op jit(solution)/shard_map/all_to_all | solution.py:327
  164.6 40.2 %collective-permute-start.5 = (bf16[4,96,1152]{2,1,0:T(8,128)(2,1)}, bf16[4,96,1152]{2,1,0:T(8,128)(2,1)}, u32[]{:S(2)}, u32[]{:S(2)}) collective-permute-start(bf16[4,96,1152]{2,1,0:T(8,128)(2,1)} %pad_maximum_fusion.1), channel_id=1, source_target_pairs={{0,4},{4,8},{8,12},{12,0},{1,5},{5,9},{9,13},{13,1},{2,6},{6,10},{... | collective-permute-start | bytes 2654216 | tf_op jit(solution)/shard_map/ppermute | solution.py:208
  167.3 37.5 %collective-permute-start.6 = (bf16[4,96,1152]{2,1,0:T(8,128)(2,1)}, bf16[4,96,1152]{2,1,0:T(8,128)(2,1)}, u32[]{:S(2)}, u32[]{:S(2)}) collective-permute-start(bf16[4,96,1152]{2,1,0:T(8,128)(2,1)} %pad_maximum_fusion.2), channel_id=1, source_target_pairs={{0,12},{4,0},{8,4},{12,8},{1,13},{5,1},{9,5},{13,9},{2,14},{6,2},{... | collective-permute-start | bytes 2654216 | tf_op jit(solution)/shard_map/ppermute | solution.py:208
  169.7 6.2 %copy-start.16 = (bf16[16,1,96,1152]{3,2,1,0:T(8,128)(2,1)S(1)}, bf16[16,1,96,1152]{3,2,1,0:T(8,128)(2,1)}, u32[]{:S(2)}) copy-start(bf16[16,1,96,1152]{3,2,1,0:T(8,128)(2,1)} %copy-done.15) | copy-start | bytes 10616836
  171.7 5.5 %copy-start.14 = (bf16[16,1,96,1152]{3,2,1,0:T(8,128)(2,1)S(1)}, bf16[16,1,96,1152]{3,2,1,0:T(8,128)(2,1)}, u32[]{:S(2)}) copy-start(bf16[16,1,96,1152]{3,2,1,0:T(8,128)(2,1)} %copy-done.13) | copy-start | bytes 10616836
  171.7 34.3 %collective-permute-start.7 = (bf16[4,96,1152]{2,1,0:T(8,128)(2,1)}, bf16[4,96,1152]{2,1,0:T(8,128)(2,1)}, u32[]{:S(2)}, u32[]{:S(2)}) collective-permute-start(bf16[4,96,1152]{2,1,0:T(8,128)(2,1)} %pad_maximum_fusion.3), channel_id=1, source_target_pairs={{0,16},{16,32},{32,48},{48,0},{1,17},{17,33},{33,49},{49,1},{2,18}... | collective-permute-start | bytes 2654216 | tf_op jit(solution)/shard_map/ppermute | solution.py:208
  174.4 31.6 %collective-permute-start.8 = (bf16[4,96,1152]{2,1,0:T(8,128)(2,1)}, bf16[4,96,1152]{2,1,0:T(8,128)(2,1)}, u32[]{:S(2)}, u32[]{:S(2)}) collective-permute-start(bf16[4,96,1152]{2,1,0:T(8,128)(2,1)} %pad_maximum_fusion.4), channel_id=1, source_target_pairs={{0,48},{16,0},{32,16},{48,32},{1,49},{17,1},{33,17},{49,33},{2,50}... | collective-permute-start | bytes 2654216 | tf_op jit(solution)/shard_map/ppermute | solution.py:208
  198.6 13.8 %copy-start.31 = (bf16[4,96,768]{2,1,0:T(8,128)(2,1)S(1)}, bf16[4,96,768]{2,1,0:T(8,128)(2,1)}, u32[]{:S(2)}) copy-start(bf16[4,96,768]{2,1,0:T(8,128)(2,1)} %get-tuple-element.90) | copy-start | bytes 1769476
  206.0 14.5 %all-to-all-start.4 = ((bf16[4,160,512]{2,1,0:T(8,128)(2,1)}), bf16[4,160,512]{2,1,0:T(8,128)(2,1)}, u32[]{:S(2)}, u32[]{:S(2)}) async-start(bf16[4,160,512]{2,1,0:T(8,128)(2,1)} %get-tuple-element.59), calls=%async_computation.4 | async-start | bytes 1310720 | tf_op jit(solution)/shard_map/all_to_all | solution.py:41
  214.4 26.3 %collective-permute-start.9 = (bf16[2,256,768]{2,1,0:T(8,128)(2,1)}, bf16[2,256,768]{2,1,0:T(8,128)(2,1)}, u32[]{:S(2)}, u32[]{:S(2)}) collective-permute-start(bf16[2,256,768]{2,1,0:T(8,128)(2,1)} %pad_maximum_fusion.10), channel_id=1, source_target_pairs={{0,1},{1,0},{2,3},{3,2},{4,5},{5,4},{6,7},{7,6},{8,9},{9,8},{10,11... | collective-permute-start | bytes 2359304 | tf_op jit(solution)/shard_map/ppermute | solution.py:362
  215.8 26.8 %collective-permute-start.16 = (bf16[4,96,1152]{2,1,0:T(8,128)(2,1)}, bf16[4,96,1152]{2,1,0:T(8,128)(2,1)}, u32[]{:S(2)}, u32[]{:S(2)}) collective-permute-start(bf16[4,96,1152]{2,1,0:T(8,128)(2,1)} %pad_maximum_fusion.8), channel_id=1, source_target_pairs={{0,8},{4,12},{8,0},{12,4},{1,9},{5,13},{9,1},{13,5},{2,10},{6,14},... | collective-permute-start | bytes 2654216 | tf_op jit(solution)/shard_map/ppermute | solution.py:208
  218.3 31.9 %collective-permute-start.12 = (bf16[4,96,1152]{2,1,0:T(8,128)(2,1)}, bf16[4,96,1152]{2,1,0:T(8,128)(2,1)}, u32[]{:S(2)}, u32[]{:S(2)}) collective-permute-start(bf16[4,96,1152]{2,1,0:T(8,128)(2,1)} %pad_maximum_fusion.6), channel_id=1, source_target_pairs={{0,32},{16,48},{32,0},{48,16},{1,33},{17,49},{33,1},{49,17},{2,34}... | collective-permute-start | bytes 2654216 | tf_op jit(solution)/shard_map/ppermute | solution.py:208
  220.5 8.6 %copy-start.7 = (bf16[768,640]{1,0:T(8,128)(2,1)S(1)}, bf16[768,640]{1,0:T(8,128)(2,1)}, u32[]{:S(2)}) copy-start(bf16[768,640]{1,0:T(8,128)(2,1)} %fusion.27.perm_t) | copy-start | bytes 2949124
  232.9 7.8 %copy-start.22 = (bf16[2,256,768]{2,1,0:T(8,128)(2,1)S(1)}, bf16[2,256,768]{2,1,0:T(8,128)(2,1)}, u32[]{:S(2)}) copy-start(bf16[2,256,768]{2,1,0:T(8,128)(2,1)} %pad_maximum_fusion.9) | copy-start | bytes 2359300
  232.9 9.7 %copy-start.30 = (bf16[4,96,1152]{2,1,0:T(8,128)(2,1)S(1)}, bf16[4,96,1152]{2,1,0:T(8,128)(2,1)}, u32[]{:S(2)}) copy-start(bf16[4,96,1152]{2,1,0:T(8,128)(2,1)} %pad_maximum_fusion.7) | copy-start | bytes 2654212
  232.9 53.9 %all-to-all-start.5 = ((bf16[32,24,720]{2,1,0:T(8,128)(2,1)}), bf16[32,24,720]{2,1,0:T(8,128)(2,1)}, u32[]{:S(2)}, u32[]{:S(2)}) async-start(bf16[32,24,720]{2,1,0:T(8,128)(2,1)} %bitcast.184), calls=%async_computation.5 | async-start | bytes 2359296 | tf_op jit(solution)/shard_map/all_to_all | solution.py:392
  242.0 28.1 %collective-permute-start.10 = (bf16[256,768]{1,0:T(8,128)(2,1)S(1)}, bf16[256,768]{1,0:T(8,128)(2,1)S(1)}, u32[]{:S(2)}, u32[]{:S(2)}) collective-permute-start(bf16[256,768]{1,0:T(8,128)(2,1)S(1)} %select_bitcast_fusion.2), channel_id=1, source_target_pairs={{0,2},{2,0},{1,3},{3,1},{4,6},{6,4},{5,7},{7,5},{8,10},{10,8},{9,1... | collective-permute-start | bytes 1179656 | tf_op jit(solution)/shard_map/ppermute | solution.py:367
  244.7 5.4 %copy-start.29 = (bf16[4,96,1152]{2,1,0:T(8,128)(2,1)S(1)}, bf16[4,96,1152]{2,1,0:T(8,128)(2,1)}, u32[]{:S(2)}) copy-start(bf16[4,96,1152]{2,1,0:T(8,128)(2,1)} %pad_maximum_fusion.5) | copy-start | bytes 2654212
  244.8 17.9 %collective-permute-start.17 = (bf16[96,1152]{1,0:T(8,128)(2,1)S(1)}, bf16[96,1152]{1,0:T(8,128)(2,1)S(1)}, u32[]{:S(2)}, u32[]{:S(2)}) collective-permute-start(bf16[96,1152]{1,0:T(8,128)(2,1)S(1)} %get-tuple-element.114), channel_id=1, source_target_pairs={{0,16},{16,32},{32,48},{48,0},{1,17},{17,33},{33,49},{49,1},{2,18}... | collective-permute-start | bytes 663560 | tf_op jit(solution)/shard_map/ppermute | solution.py:208
  246.6 23.5 %collective-permute-start.18 = (bf16[96,1152]{1,0:T(8,128)(2,1)S(1)}, bf16[96,1152]{1,0:T(8,128)(2,1)S(1)}, u32[]{:S(2)}, u32[]{:S(2)}) collective-permute-start(bf16[96,1152]{1,0:T(8,128)(2,1)S(1)} %get-tuple-element.113), channel_id=1, source_target_pairs={{0,48},{16,0},{32,16},{48,32},{1,49},{17,1},{33,17},{49,33},{2,50}... | collective-permute-start | bytes 663560 | tf_op jit(solution)/shard_map/ppermute | solution.py:208
  248.1 22.0 %collective-permute-start.19 = (bf16[96,1152]{1,0:T(8,128)(2,1)S(1)}, bf16[96,1152]{1,0:T(8,128)(2,1)S(1)}, u32[]{:S(2)}, u32[]{:S(2)}) collective-permute-start(bf16[96,1152]{1,0:T(8,128)(2,1)S(1)} %get-tuple-element.112), channel_id=1, source_target_pairs={{0,32},{16,48},{32,0},{48,16},{1,33},{17,49},{33,1},{49,17},{2,34}... | collective-permute-start | bytes 663560 | tf_op jit(solution)/shard_map/ppermute | solution.py:208
  252.5 28.9 %collective-permute-start.13 = (bf16[96,1152]{1,0:T(8,128)(2,1)S(1)}, bf16[96,1152]{1,0:T(8,128)(2,1)S(1)}, u32[]{:S(2)}, u32[]{:S(2)}) collective-permute-start(bf16[96,1152]{1,0:T(8,128)(2,1)S(1)} %get-tuple-element.110), channel_id=1, source_target_pairs={{0,4},{4,8},{8,12},{12,0},{1,5},{5,9},{9,13},{13,1},{2,6},{6,10},{... | collective-permute-start | bytes 663560 | tf_op jit(solution)/shard_map/ppermute | solution.py:208
  258.4 11.7 %copy-start.23 = (bf16[2,256,768]{2,1,0:T(8,128)(2,1)S(1)}, bf16[2,256,768]{2,1,0:T(8,128)(2,1)}, u32[]{:S(2)}) copy-start(bf16[2,256,768]{2,1,0:T(8,128)(2,1)} %pad_maximum_fusion.9) | copy-start | bytes 2359300
  261.0 19.9 %copy-start.36 = (pred[720,768]{1,0:T(8,128)(4,1)S(1)}, pred[720,768]{1,0:T(8,128)(4,1)}, u32[]{:S(2)}) copy-start(pred[720,768]{1,0:T(8,128)(4,1)} %copy-done.35) | copy-start | bytes 1658884
  262.7 18.7 %collective-permute-start.14 = (bf16[96,1152]{1,0:T(8,128)(2,1)S(1)}, bf16[96,1152]{1,0:T(8,128)(2,1)S(1)}, u32[]{:S(2)}, u32[]{:S(2)}) collective-permute-start(bf16[96,1152]{1,0:T(8,128)(2,1)S(1)} %get-tuple-element.109), channel_id=1, source_target_pairs={{0,12},{4,0},{8,4},{12,8},{1,13},{5,1},{9,5},{13,9},{2,14},{6,2},{... | collective-permute-start | bytes 663560 | tf_op jit(solution)/shard_map/ppermute | solution.py:208
  271.5 9.4 %collective-permute-start.11 = (bf16[128,768]{1,0:T(8,128)(2,1)S(1)}, bf16[128,768]{1,0:T(8,128)(2,1)S(1)}, u32[]{:S(2)}, u32[]{:S(2)}) collective-permute-start(bf16[128,768]{1,0:T(8,128)(2,1)S(1)} %constant_dynamic-slice_fusion), channel_id=1, source_target_pairs={{0,64},{64,0},{1,65},{65,1},{2,66},{66,2},{3,67},{67,3},{4,68},{68... | collective-permute-start | bytes 589832 | tf_op jit(solution)/shard_map/ppermute | solution.py:54
  271.8 12.7 %collective-permute-start.20 = (bf16[96,1152]{1,0:T(8,128)(2,1)S(1)}, bf16[96,1152]{1,0:T(8,128)(2,1)S(1)}, u32[]{:S(2)}, u32[]{:S(2)}) collective-permute-start(bf16[96,1152]{1,0:T(8,128)(2,1)S(1)} %add_convert_fusion.4), channel_id=1, source_target_pairs={{0,64},{64,0},{1,65},{65,1},{2,66},{66,2},{3,67},{67,3},{4,68},{68... | collective-permute-start | bytes 663560 | tf_op jit(solution)/shard_map/ppermute | solution.py:54
  275.3 8.1 %collective-permute-start.15 = (bf16[96,1152]{1,0:T(8,128)(2,1)S(1)}, bf16[96,1152]{1,0:T(8,128)(2,1)S(1)}, u32[]{:S(2)}, u32[]{:S(2)}) collective-permute-start(bf16[96,1152]{1,0:T(8,128)(2,1)S(1)} %get-tuple-element.68), channel_id=1, source_target_pairs={{0,8},{4,12},{8,0},{12,4},{1,9},{5,13},{9,1},{13,5},{2,10},{6,14},... | collective-permute-start | bytes 663560 | tf_op jit(solution)/shard_map/ppermute | solution.py:208
  281.4 5.4 %copy-start.39 = (s32[128]{0:T(128)S(1)}, s32[128]{0:T(128)}, u32[]{:S(2)}) copy-start(s32[128]{0:T(128)} %copy-done.38) | copy-start | bytes 1540
  281.4 5.4 %copy-start.41 = (s32[128]{0:T(128)S(1)}, s32[128]{0:T(128)}, u32[]{:S(2)}) copy-start(s32[128]{0:T(128)} %copy-done.40) | copy-start | bytes 1540
  (27 other events, 73.8 us)
Sparse Core Ops, SparseCore 0:
  19.1 73.7 all-gather.3
